TPU v7x, 256 devices: a whole 4x4x8 slice. The times are simulated.
256 devices in a mesh: row: 8 (over y, z_lo), col: 8 (over z_hi, core), kern: 4 (over x).
Axes of the slice: x: 4, y: 4, z: 8 (z_hi: 4, z_lo: 2; z = z_hi * 2 + z_lo), core: 2. Of those that a mesh axis runs over, the one named last changes fastest.
Arguments:
- photomask: float32 [2048, 2048], P('row', 'col'), may hold values from 0 to 1
- target_bits: int32 [2048, 2048], P('row', 'col'), may hold values 0 or 1
- active_blocks: int32 [32, 32], P('row', 'col'), may hold values 0 or 1
- kernel_taps: float32 [2, 12, 257, 257], P(None, 'kern'), may hold values from -0.0234375 to 0.0234375
- kernel_weights: float32 [12], P('kern'), may hold values from 0.1 to 1
Outputs:
- gradient: float32 [2048, 2048], P(('row', 'kern'), 'col')
- resist: float32 [2048, 2048], P('row', 'col')
All inputs are finite; a program needn't handle non-finite values. No bound on the sum of `target_bits` or of `active_blocks` on one device may be relied on, other than what follows from the above.
Results may differ from a plain program's by a relative error of at most 0.00011.
Values sent between devices are 32-bit elements; how exact they have to be, the bound alone decides.
A program may use at most 128 MiB of HBM per device.

v0:
```python
import jax
import jax.numpy as jnp
from jax import lax
from jax.sharding import PartitionSpec as P

BLK = 64


steepness = 8.0
threshold = 0.25


def with_halo(value, sides, width):
    for axis, dim in sides:
        count, length = (lax.axis_size(axis), value.shape[dim])
        up = [(i, (i + 1) % count) for i in range(count - 1)]
        down = [(j, i) for i, j in up]
        last = lax.slice_in_dim(value, length - width, length, axis=dim)
        first = lax.slice_in_dim(value, 0, width, axis=dim)
        before = lax.ppermute(last, axis, up)
        after = lax.ppermute(first, axis, down)
        value = jnp.concatenate([before, value, after], axis=dim)
    return value


def phases(first, second, length):
    turns = first[:, None] * second[None, :] % length
    angle = 2.0 * jnp.pi / length * turns.astype(jnp.float32)
    return (jnp.cos(angle), jnp.sin(angle))


def matmul_high(left_side, right_side):
    return jnp.dot(
        left_side, right_side, precision=lax.Precision.HIGHEST, preferred_element_type=jnp.float32
    )


def left_apply(table, stack):
    return jnp.einsum("ab,kbc->kac", table, stack, precision=lax.Precision.HIGHEST)


def right_apply(stack, table):
    return jnp.einsum("kab,bc->kac", stack, table, precision=lax.Precision.HIGHEST)


def respond(intensity, target_bits):
    resist = jax.nn.sigmoid(steepness * (intensity - threshold))
    factor = 2.0 * (resist - target_bits.astype(jnp.float32)) * steepness * resist * (1.0 - resist)
    return (resist, factor)


def local(photomask, target_bits, active_blocks, kernel_taps, kernel_weights):
    tile_rows, tile_cols = photomask.shape
    groups = kernel_taps.shape[1]
    groups_count = lax.axis_size("kern")
    total_kernels = groups * groups_count
    kernel_span = kernel_taps.shape[-1]
    radius = kernel_span // 2
    padded_rows = tile_rows + 2 * radius
    padded_cols = tile_cols + 2 * radius
    inverse_count = 1.0 / (padded_rows * padded_cols)
    row_freq = jnp.arange(padded_rows, dtype=jnp.int32)
    col_freq = jnp.arange(padded_cols, dtype=jnp.int32)
    full_row_cos, full_row_sin = phases(row_freq, row_freq, padded_rows)
    full_col_cos, full_col_sin = phases(col_freq, col_freq, padded_cols)
    tile_row_cos, tile_row_sin = phases(
        radius + jnp.arange(tile_rows, dtype=jnp.int32), row_freq, padded_rows
    )
    tile_col_cos, tile_col_sin = phases(
        col_freq, radius + jnp.arange(tile_cols, dtype=jnp.int32), padded_cols
    )
    offsets = jnp.arange(kernel_span, dtype=jnp.int32) - radius
    tap_col_cos, tap_col_sin = phases(offsets % padded_cols, col_freq, padded_cols)
    tap_row_cos, tap_row_sin = phases(row_freq, offsets % padded_rows, padded_rows)
    padded = with_halo(photomask, (("row", 0), ("col", 1)), radius)
    col_real = matmul_high(padded, full_col_cos)
    col_imag = -matmul_high(padded, full_col_sin)
    mask_real = matmul_high(full_row_cos, col_real) + matmul_high(full_row_sin, col_imag)
    mask_imag = matmul_high(full_row_cos, col_imag) - matmul_high(full_row_sin, col_real)
    taps_real = kernel_taps[0]
    taps_imag = kernel_taps[1]
    half_real = right_apply(taps_real, tap_col_cos) - right_apply(taps_imag, tap_col_sin)
    half_imag = right_apply(taps_real, tap_col_sin) + right_apply(taps_imag, tap_col_cos)
    response_real = left_apply(tap_row_cos, half_real) - left_apply(tap_row_sin, half_imag)
    response_imag = left_apply(tap_row_cos, half_imag) + left_apply(tap_row_sin, half_real)
    spec_real = mask_real[None] * response_real - mask_imag[None] * response_imag
    spec_imag = mask_real[None] * response_imag + mask_imag[None] * response_real
    band_real = left_apply(tile_row_cos, spec_real) - left_apply(tile_row_sin, spec_imag)
    band_imag = left_apply(tile_row_cos, spec_imag) + left_apply(tile_row_sin, spec_real)
    amp_real = (
        right_apply(band_real, tile_col_cos) - right_apply(band_imag, tile_col_sin)
    ) * inverse_count
    amp_imag = (
        right_apply(band_real, tile_col_sin) + right_apply(band_imag, tile_col_cos)
    ) * inverse_count
    weighted = kernel_weights[:, None, None] * (amp_real * amp_real + amp_imag * amp_imag)
    partial_value = jnp.sum(weighted, axis=0) / total_kernels
    intensity = lax.psum(partial_value, "kern")
    resist, factor = respond(intensity, target_bits)
    coefficient = 2.0 / total_kernels * kernel_weights[:, None, None]
    product_real = factor[None] * coefficient * amp_real
    product_imag = factor[None] * coefficient * amp_imag
    stacked = jnp.stack([product_real, product_imag])
    wide = with_halo(stacked, (("row", 2), ("col", 3)), radius)
    wide_real = wide[0]
    wide_imag = wide[1]
    cols_real = right_apply(wide_real, full_col_cos) + right_apply(wide_imag, full_col_sin)
    cols_imag = right_apply(wide_imag, full_col_cos) - right_apply(wide_real, full_col_sin)
    freq_real = left_apply(full_row_cos, cols_real) + left_apply(full_row_sin, cols_imag)
    freq_imag = left_apply(full_row_cos, cols_imag) - left_apply(full_row_sin, cols_real)
    summed_real = jnp.sum(freq_real * response_real + freq_imag * response_imag, axis=0)
    summed_imag = jnp.sum(freq_imag * response_real - freq_real * response_imag, axis=0)
    back_real = matmul_high(tile_row_cos, summed_real) - matmul_high(tile_row_sin, summed_imag)
    back_imag = matmul_high(tile_row_cos, summed_imag) + matmul_high(tile_row_sin, summed_real)
    term = (
        matmul_high(back_real, tile_col_cos) - matmul_high(back_imag, tile_col_sin)
    ) * inverse_count
    gradient_share = lax.psum_scatter(term, "kern", scatter_dimension=0, tiled=True)
    block_rows, block_cols = active_blocks.shape
    expanded = jnp.broadcast_to(active_blocks[:, None, :, None], (block_rows, BLK, block_cols, BLK))
    pixels = expanded.reshape(tile_rows, tile_cols).astype(jnp.float32)
    share_count = tile_rows // groups_count
    pixel_share = lax.dynamic_slice_in_dim(
        pixels, lax.axis_index("kern") * share_count, share_count, 0
    )
    return (gradient_share * pixel_share, resist)


def solution(mesh):
    in_specs = (
        P("row", "col"),
        P("row", "col"),
        P("row", "col"),
        P(None, "kern", None, None),
        P("kern"),
    )
    out_specs = (P(("row", "kern"), "col"), P("row", "col"))
    return jax.shard_map(local, mesh=mesh, in_specs=in_specs, out_specs=out_specs, check_vma=False)
```

profile of v0, /device:TPU:8, one launch (start us, length us, event | category | flops | bytes accessed | tf_op | source)
XLA Modules:
  0.0 450.7 jit_solution(9010044798153330881)
XLA Ops:
  34.1 7.3 %fusion.16 = f32[3,512,512]{2,1,0:T(8,128)S(1)} fusion(f32[512,3,257]{0,2,1:T(8,128)S(1)} %convolution_subtract_fusion.2, s32[257]{0:T(512)S(1)} %add_select_fusion.5), kind=kOutput, calls=%fused_computation.32 | convolution fusion | flops 2427198464 | bytes 4725764 | tf_op jit(solution)/shard_map/ab,kbc->kac/dot_general | solution.py:39
  46.3 7.2 %convolution_subtract_fusion.1 = f32[3,512,512]{2,1,0:T(8,128)S(1)} fusion(f32[3,512,512]{2,1,0:T(8,128)S(1)} %fusion.16, f32[512,3,257]{0,2,1:T(8,128)S(1)} %convolution_add_fusion.2, s32[257]{0:T(512)S(1)} %add_select_fusion.5), kind=kOutput, calls=%fused_computation.27 | convolution fusion | flops 2427984896 | bytes 7871492 | tf_op jit(solution)/shard_map/ab,kbc->kac/dot_general | solution.py:39
  53.5 7.7 %fusion.12 = f32[3,512,512]{2,1,0:T(8,128)S(1)} fusion(f32[512,3,257]{0,2,1:T(8,128)S(1)} %convolution_add_fusion.2, s32[257]{0:T(512)S(1)} %add_select_fusion.5), kind=kOutput, calls=%fused_computation.28 | convolution fusion | flops 2427198464 | bytes 4725764 | tf_op jit(solution)/shard_map/ab,kbc->kac/dot_general | solution.py:39
  63.9 8.8 %convolution_add_fusion.1 = f32[3,512,512]{2,1,0:T(8,128)} fusion(f32[3,512,512]{2,1,0:T(8,128)S(1)} %fusion.12, f32[512,3,257]{0,2,1:T(8,128)S(1)} %convolution_subtract_fusion.2, s32[257]{0:T(512)S(1)} %add_select_fusion.5), kind=kOutput, calls=%fused_computation.26 | convolution fusion | flops 2427984896 | bytes 7871492 | tf_op jit(solution)/shard_map/ab,kbc->kac/dot_general | solution.py:39
  72.7 5.9 %fusion.60 = f32[512,512]{1,0:T(8,128)S(1)} fusion(f32[512,128]{1,0:T(8,128)S(1)} %collective-permute-done.3, f32[512,256]{1,0:T(8,128)S(1)} %constant_dynamic-update-slice_fusion, f32[512,128]{1,0:T(8,128)S(1)} %collective-permute-done.2), kind=kOutput, calls=%fused_computation.102 | convolution fusion | flops 1614807040 | bytes 2097152 | tf_op jit(solution)/shard_map/dot_general | solution.py:33
  78.6 5.7 %fusion.107 = f32[512,512]{1,0:T(8,128)S(1)} fusion(f32[512,512]{1,0:T(8,128)S(1)} %fusion.60), kind=kOutput, calls=%fused_computation.144 | convolution fusion | flops 1614282752 | bytes 2097152 | tf_op jit(solution)/shard_map/dot_general | solution.py:33
  84.3 5.9 %convolution_negate_fusion = f32[512,512]{1,0:T(8,128)S(1)} fusion(f32[512,128]{1,0:T(8,128)S(1)} %collective-permute-done.3, f32[512,256]{1,0:T(8,128)S(1)} %constant_dynamic-update-slice_fusion, f32[512,128]{1,0:T(8,128)S(1)} %collective-permute-done.2), kind=kOutput, calls=%fused_computation.53 | convolution fusion | flops 1615069184 | bytes 2097152 | tf_op jit(solution)/shard_map/dot_general | solution.py:33
  90.3 6.9 %fusion.105 = f32[512,512]{1,0:T(8,128)} fusion(f32[512,512]{1,0:T(8,128)S(1)} %convolution_negate_fusion), kind=kOutput, calls=%fused_computation.143 | convolution fusion | flops 1614282752 | bytes 2097152 | tf_op jit(solution)/shard_map/dot_general | solution.py:33
  97.2 6.9 %convolution_add_fusion.4 = f32[512,512]{1,0:T(8,128)} fusion(f32[512,512]{1,0:T(8,128)S(1)} %fusion.107, f32[512,512]{1,0:T(8,128)S(1)} %convolution_negate_fusion), kind=kOutput, calls=%fused_computation.52 | convolution fusion | flops 1614544896 | bytes 3145728 | tf_op jit(solution)/shard_map/dot_general | solution.py:33
  106.6 8.7 %convolution_subtract_fusion.4 = f32[512,512]{1,0:T(8,128)} fusion(f32[512,512]{1,0:T(8,128)} %fusion.105, f32[512,512]{1,0:T(8,128)} %copy-done.9), kind=kOutput, calls=%fused_computation.51 | convolution fusion | flops 1614544896 | bytes 3145728 | tf_op jit(solution)/shard_map/dot_general | solution.py:33
  117.8 7.5 %fusion.95 = f32[3,512,256]{2,1,0:T(8,128)S(1)} fusion(s32[256]{0:T(256)S(1)} %iota_add_fusion, f32[3,512,512]{2,1,0:T(8,128)} %convolution_add_fusion.1, f32[3,512,512]{2,1,0:T(8,128)S(1)} %convolution_subtract_fusion.1, f32[512,512]{0,1:T(8,128)} %copy.22, f32[512,512]{0,1:T(8,128)} %copy.19), kind=kOutput, calls=%fused_computation.137 | convolution fusion | flops 2420113408 | bytes 9962496 | tf_op jit(solution)/shard_map/ab,kbc->kac/dot_general | solution.py:39
  153.7 5.5 %multiply_reduce_fusion = (f32[256,256]{1,0:T(8,128)S(1)}, f32[3,256,256]{2,1,0:T(8,128)}) fusion(f32[3,256,256]{2,1,0:T(8,128)S(1)} %fusion.29, f32[3]{0:T(128)S(1)} %copy-done.8, f32[3,256,256]{2,1,0:T(8,128)S(1)} %fusion.18, s32[256]{0:T(256)S(1)} %iota_add_fusion, f32[3,512,256]{2,1,0:T(8,128)S(1)} %convolution_subtract_fusion.3), kind=kOutput, calls=%fused_computation.95 | convolution fusion | flops 1211105280 | bytes 4195340 | tf_op jit(solution)/shard_map/kab,bc->kac/dot_general | solution.py:43
  160.0 54.8 %all-reduce.2.cloned.1.call-done = f32[256,256]{1,0:T(8,128)} async-done(((f32[256,256]{1,0:T(8,128)}), f32[256,256]{1,0:T(8,128)}) %all-reduce.2.cloned.1.call-update) | async-done | bytes 262160 | tf_op jit(solution)/shard_map/psum | solution.py:98
  225.1 16.5 %collective-permute-done.4 = f32[2,3,128,256]{3,2,1,0:T(8,128)S(1)} collective-permute-done((f32[2,3,128,256]{3,2,1,0:T(8,128)S(1)}, f32[2,3,128,256]{3,2,1,0:T(8,128)S(1)}, u32[]{:S(2)}, u32[]{:S(2)}) %collective-permute-start.4) | collective-permute-done | bytes 786464 | tf_op jit(solution)/shard_map/ppermute | solution.py:20
  241.6 13.5 %collective-permute-done.5 = f32[2,3,128,256]{3,2,1,0:T(8,128)S(1)} collective-permute-done((f32[2,3,128,256]{3,2,1,0:T(8,128)S(1)}, f32[2,3,128,256]{3,2,1,0:T(8,128)S(1)}, u32[]{:S(2)}, u32[]{:S(2)}) %collective-permute-start.5) | collective-permute-done | bytes 786464 | tf_op jit(solution)/shard_map/ppermute | solution.py:21
  265.9 9.0 %fusion.6 = f32[3,512,512]{2,1,0:T(8,128)S(1)} fusion(f32[2,3,512,512]{3,2,1,0:T(8,128)S(1)} %pad_maximum_fusion), kind=kOutput, calls=%fused_computation.18 | convolution fusion | flops 4835508224 | bytes 6291456 | tf_op jit(solution)/shard_map/kab,bc->kac/dot_general | solution.py:43
  274.9 9.6 %fusion.9 = f32[3,512,512]{2,1,0:T(8,128)S(1)} fusion(f32[2,3,512,512]{3,2,1,0:T(8,128)S(1)} %pad_maximum_fusion), kind=kOutput, calls=%fused_computation.21 | convolution fusion | flops 4835508224 | bytes 6291456 | tf_op jit(solution)/shard_map/kab,bc->kac/dot_general | solution.py:43
  284.5 9.4 %fusion.10 = f32[3,512,512]{2,1,0:T(8,128)S(1)} fusion(f32[3,512,512]{2,1,0:T(8,128)S(1)} %fusion.6, f32[2,3,512,512]{3,2,1,0:T(8,128)S(1)} %pad_maximum_fusion), kind=kOutput, calls=%fused_computation.22 | convolution fusion | flops 4836294656 | bytes 9437184 | tf_op jit(solution)/shard_map/kab,bc->kac/dot_general | solution.py:43
  294.0 9.1 %fusion.11 = f32[3,512,512]{2,1,0:T(8,128)S(1)} fusion(f32[3,512,512]{2,1,0:T(8,128)S(1)} %fusion.9, f32[2,3,512,512]{3,2,1,0:T(8,128)S(1)} %pad_maximum_fusion), kind=kOutput, calls=%fused_computation.23 | convolution fusion | flops 4836294656 | bytes 9437184 | tf_op jit(solution)/shard_map/kab,bc->kac/dot_general | solution.py:43
  303.1 15.8 %fusion.51 = f32[3,512,512]{2,1,0:T(8,128)S(1)} fusion(f32[3,512,512]{2,1,0:T(8,128)S(1)} %fusion.11), kind=kOutput, calls=%fused_computation.79 | convolution fusion | flops 4835508224 | bytes 6291456 | tf_op jit(solution)/shard_map/ab,kbc->kac/dot_general | solution.py:39
  318.9 16.0 %fusion.48 = f32[3,512,512]{2,1,0:T(8,128)S(1)} fusion(f32[3,512,512]{2,1,0:T(8,128)S(1)} %fusion.10), kind=kOutput, calls=%fused_computation.76 | convolution fusion | flops 4835508224 | bytes 6291456 | tf_op jit(solution)/shard_map/ab,kbc->kac/dot_general | solution.py:39
  334.9 16.1 %convolution_add_fusion = f32[3,512,512]{2,1,0:T(8,128)S(1)} fusion(f32[3,512,512]{2,1,0:T(8,128)S(1)} %fusion.51, f32[3,512,512]{2,1,0:T(8,128)S(1)} %fusion.10), kind=kOutput, calls=%fused_computation.25 | convolution fusion | flops 4836294656 | bytes 9437184 | tf_op jit(solution)/shard_map/ab,kbc->kac/dot_general | solution.py:39
  351.1 15.2 %fusion.3 = (f32[512,512]{0,1:T(8,128)S(1)}, f32[512,512]{0,1:T(8,128)S(1)}) fusion(f32[3,512,512]{2,1,0:T(8,128)S(1)} %convolution_add_fusion, f32[3,512,512]{2,1,0:T(8,128)S(1)} %copy-done.1, f32[3,512,512]{2,1,0:T(8,128)S(1)} %convolution_subtract_fusion.1, f32[3,512,512]{2,1,0:T(8,128)S(1)} %fusion.48, f32[3,512,512]{2,1,0:T(8,128)S(1)} %fusion.11), kind=kOutput, calls=%fused_computation.9 | convolution fusion | flops 4842061824 | bytes 17825792 | tf_op jit(solution)/shard_map/ab,kbc->kac/dot_general | solution.py:39
  385.0 56.9 %reduce-scatter.2.cloned.1.call-done = f32[64,256]{1,0:T(8,128)} async-done(((f32[256,256]{1,0:T(8,128)}), f32[64,256]{1,0:T(8,128)}) %reduce-scatter.2.cloned.1.call-update) | async-done | bytes 65552 | tf_op jit(solution)/shard_map/reduce_scatter | solution.py:118
  (76 shorter events, 109.7 us)
Async XLA Ops:
  7.2 207.7 %all-reduce.2.cloned.1.call-start = ((), (), s32[]{:S(2)}) async-start(), calls=%async_computation.1 | async-start | bytes 524288 | tf_op jit(solution)/shard_map/psum | solution.py:98
  8.2 52.9 %collective-permute-start = (f32[128,256]{1,0:T(8,128)S(1)}, f32[128,256]{1,0:T(8,128)S(1)}, u32[]{:S(2)}, u32[]{:S(2)}) collective-permute-start(f32[128,256]{1,0:T(8,128)S(1)} %get-tuple-element.17), channel_id=1, source_target_pairs={{0,32},{32,64},{64,96},{96,128},{128,160},{160,192},{192,224},{1,3... | collective-permute-start | bytes 393224 | tf_op jit(solution)/shard_map/ppermute | solution.py:20
  12.0 49.2 %collective-permute-start.1 = (f32[128,256]{1,0:T(8,128)S(1)}, f32[128,256]{1,0:T(8,128)S(1)}, u32[]{:S(2)}, u32[]{:S(2)}) collective-permute-start(f32[128,256]{1,0:T(8,128)S(1)} %get-tuple-element.16), channel_id=1, source_target_pairs={{32,0},{64,32},{96,64},{128,96},{160,128},{192,160},{224,192},{33,... | collective-permute-start | bytes 393224 | tf_op jit(solution)/shard_map/ppermute | solution.py:21
  53.5 7.7 %copy-start.5 = (f32[256,256]{1,0:T(8,128)S(1)}, f32[256,256]{1,0:T(8,128)}, u32[]{:S(2)}) copy-start(f32[256,256]{1,0:T(8,128)} %param.5) | copy-start | bytes 786436
  61.3 11.5 %collective-permute-start.2 = (f32[512,128]{1,0:T(8,128)S(1)}, f32[512,128]{1,0:T(8,128)S(1)}, u32[]{:S(2)}, u32[]{:S(2)}) collective-permute-start(f32[512,128]{1,0:T(8,128)S(1)} %get-tuple-element.12), channel_id=1, source_target_pairs={{0,4},{4,8},{8,12},{12,16},{16,20},{20,24},{24,28},{1,5},{5,9},{9,... | collective-permute-start | bytes 786440 | tf_op jit(solution)/shard_map/ppermute | solution.py:20
  62.6 10.1 %collective-permute-start.3 = (f32[512,128]{1,0:T(8,128)S(1)}, f32[512,128]{1,0:T(8,128)S(1)}, u32[]{:S(2)}, u32[]{:S(2)}) collective-permute-start(f32[512,128]{1,0:T(8,128)S(1)} %get-tuple-element.13), channel_id=1, source_target_pairs={{4,0},{8,4},{12,8},{16,12},{20,16},{24,20},{28,24},{5,1},{9,5},{13... | collective-permute-start | bytes 786440 | tf_op jit(solution)/shard_map/ppermute | solution.py:21
  78.6 11.7 %copy-start.9 = (f32[512,512]{1,0:T(8,128)}, f32[512,512]{1,0:T(8,128)S(1)}, u32[]{:S(2)}) copy-start(f32[512,512]{1,0:T(8,128)S(1)} %fusion.60) | copy-start | bytes 3145732
  117.8 7.5 %copy-start = (f32[3,512,512]{2,1,0:T(8,128)S(1)}, f32[3,512,512]{2,1,0:T(8,128)}, u32[]{:S(2)}) copy-start(f32[3,512,512]{2,1,0:T(8,128)} %convolution_add_fusion.1) | copy-start | bytes 9437188
  117.8 7.5 %copy-start.2 = (f32[512,512]{0,1:T(8,128)S(1)}, f32[512,512]{0,1:T(8,128)}, u32[]{:S(2)}) copy-start(f32[512,512]{0,1:T(8,128)} %copy.19) | copy-start | bytes 3145732
  117.8 7.5 %copy-start.3 = (f32[512,512]{0,1:T(8,128)S(1)}, f32[512,512]{0,1:T(8,128)}, u32[]{:S(2)}) copy-start(f32[512,512]{0,1:T(8,128)} %copy.22) | copy-start | bytes 3145732
  149.2 4.4 copy-start.8
  153.7 5.6 %copy-start.4 = (f32[3,256,256]{2,1,0:T(8,128)}, f32[3,256,256]{2,1,0:T(8,128)S(1)}, u32[]{:S(2)}) copy-start(f32[3,256,256]{2,1,0:T(8,128)S(1)} %fusion.29) | copy-start | bytes 2359300
  153.7 61.2 %copy-start.6 = (s32[256,256]{1,0:T(8,128)S(1)}, s32[256,256]{1,0:T(8,128)}, u32[]{:S(2)}) copy-start(s32[256,256]{1,0:T(8,128)} %param.6) | copy-start | bytes 786436
  160.0 282.0 %reduce-scatter.2.cloned.1.call-start = ((), (), s32[]{:S(2)}) async-start(), calls=%async_computation.2 | async-start | bytes 327680 | tf_op jit(solution)/shard_map/reduce_scatter | solution.py:118
  218.3 23.3 %collective-permute-start.4 = (f32[2,3,128,256]{3,2,1,0:T(8,128)S(1)}, f32[2,3,128,256]{3,2,1,0:T(8,128)S(1)}, u32[]{:S(2)}, u32[]{:S(2)}) collective-permute-start(f32[2,3,128,256]{3,2,1,0:T(8,128)S(1)} %get-tuple-element.10), channel_id=1, source_target_pairs={{0,32},{32,64},{64,96},{96,128},{128,160},{160,192},{192,224},{1,3... | collective-permute-start | bytes 2359304 | tf_op jit(solution)/shard_map/ppermute | solution.py:20
  221.8 33.3 %collective-permute-start.5 = (f32[2,3,128,256]{3,2,1,0:T(8,128)S(1)}, f32[2,3,128,256]{3,2,1,0:T(8,128)S(1)}, u32[]{:S(2)}, u32[]{:S(2)}) collective-permute-start(f32[2,3,128,256]{3,2,1,0:T(8,128)S(1)} %get-tuple-element.11), channel_id=1, source_target_pairs={{32,0},{64,32},{96,64},{128,96},{160,128},{192,160},{224,192},{33,... | collective-permute-start | bytes 2359304 | tf_op jit(solution)/shard_map/ppermute | solution.py:21
  255.8 4.3 collective-permute-start.6
  257.2 8.0 %collective-permute-start.7 = (f32[2,3,512,128]{3,2,1,0:T(8,128)S(1)}, f32[2,3,512,128]{3,2,1,0:T(8,128)S(1)}, u32[]{:S(2)}, u32[]{:S(2)}) collective-permute-start(f32[2,3,512,128]{3,2,1,0:T(8,128)S(1)} %get-tuple-element.7), channel_id=1, source_target_pairs={{4,0},{8,4},{12,8},{16,12},{20,16},{24,20},{28,24},{5,1},{9,5},{13... | collective-permute-start | bytes 4718600 | tf_op jit(solution)/shard_map/ppermute | solution.py:21
  334.9 16.2 %copy-start.1 = (f32[3,512,512]{2,1,0:T(8,128)S(1)}, f32[3,512,512]{2,1,0:T(8,128)}, u32[]{:S(2)}) copy-start(f32[3,512,512]{2,1,0:T(8,128)} %convolution_add_fusion.1) | copy-start | bytes 9437188
  378.5 6.1 %copy-start.7 = (s32[4,4]{1,0:T(4,128)S(1)}, s32[4,4]{1,0:T(4,128)}, u32[]{:S(2)}) copy-start(s32[4,4]{1,0:T(4,128)} %param.7) | copy-start | bytes 196
Sparse Core Ops, SparseCore 0:
  160.1 54.6 all-reduce.1
  384.6 57.2 reduce-scatter.1
where the time goes:
time: 460 us; the launch traced here: 451 us
  matrix products  250 us (54%)
  waiting for transfers between devices  148 us (32%)
  starting transfers between devices  18.8 us (4%)
  between operations  15 us (3%)
  local copies, waits for them, and re-layouts  11.4 us (2%)
  other arithmetic  6.74 us (1%)
    dot_general x12, matrix products, left_apply(): jnp.einsum('ab,kbc->kac', table, stack, precision=lax.Precision.HIGHEST)  116 us
    dot_general x12, matrix products, right_apply(): jnp.einsum('kab,bc->kac', stack, table, precision=lax.Precision.HIGHEST)  75.9 us
    dot_general x12, matrix products, matmul_high(): jnp.dot(left_side, right_side, precision=lax.Precision.HIGHEST, preferred...  58.1 us
    reduce_scatter x1, waiting for transfers between devices, local(): lax.psum_scatter(term, 'kern', scatter_dimension=0, tiled=True)  56.9 us
    psum x1, waiting for transfers between devices, local(): intensity = lax.psum(partial_value, 'kern')  54.8 us
    ppermute x4, waiting for transfers between devices, with_halo(): after = lax.ppermute(first, axis, down)  18.6 us
    ppermute x4, waiting for transfers between devices, with_halo(): before = lax.ppermute(last, axis, up)  18.1 us
    ppermute x4, starting transfers between devices, with_halo(): before = lax.ppermute(last, axis, up)  9.98 us
  transfers between devices with their start and end apart: 10, of which 6 were waited for; matrix products, arithmetic and copies ran while one was open for 12% of the time, Pallas kernels for 0%

commit v1 on v0

v1 whole, which is shorter than its diff:
```python
import functools

import jax
import jax.numpy as jnp
import numpy as np
from jax import lax
from jax.experimental import pallas as pl
from jax.experimental.pallas import tpu as pltpu
from jax.sharding import PartitionSpec as P

MESH = pl.DeviceIdType.MESH
T = 256
W = 512
R = 128
PARTS = 6
Q = 64
SCALE = 2.0 ** -17
F32 = jnp.float32
BF = jnp.bfloat16


def tables():
    sample = np.arange(W)[:, None]
    freq = np.arange(T)[None, :]
    angle = np.pi / W * (sample * (2 * freq + 1) % (2 * W))
    cos, sin = np.cos(angle), np.sin(angle)
    full = np.concatenate([cos[:, :R], sin[:, :R], cos[:, R:], sin[:, R:]], axis=1)
    full[np.abs(full) < 1e-12] = 0.0
    high = full.astype(BF)
    low = (full - high.astype(np.float64)).astype(BF)
    return high, low, np.ascontiguousarray(high.T), np.ascontiguousarray(low.T)


def split(value):
    high = value.astype(BF)
    return high, (value - high.astype(F32)).astype(BF)


def dot(a, b):
    return jnp.dot(a, b, preferred_element_type=F32)


def dot3(ah, al, bh, bl):
    return dot(ah, bh) + dot(al, bh) + dot(ah, bl)


def to_complex(block):
    cc, cs = block[:R, :R], block[:R, R:]
    sc, ss = block[R:, :R], block[R:, R:]
    return cc - ss, -(cs + sc), cc + ss, cs - sc


def from_complex(pr, pi, mr, mi):
    return pr + mr, mi - pi, -(pi + mi), mr - pr


def kernel(
    mask, target, active, taps, weights, rh_in, rl_in, th_in, tl_in,
    gradient, resist,
    win, tapv, rh, rl, th, tl, targ, taph, rhat, xh, xl, hs, ms, vh, vl, amp, ph, pw,
    ipart, irecv, resv, acc, tsend, trecv, fsend, frecv, gw, erecv, outv,
    lsem, msend, mrecv, isend, isem, asend, asem, tss, trs, fss, frs, ess, ers,
):
    r, c, j = lax.axis_index("row"), lax.axis_index("col"), lax.axis_index("kern")
    rows, cols = lax.axis_size("row"), lax.axis_size("col")
    has = (r > 0, r < rows - 1, c > 0, c < cols - 1)
    where = ({"row": r - 1}, {"row": r + 1}, {"col": c - 1}, {"col": c + 1})
    peer = [lax.rem(j + d, 4) for d in range(4)]

    loads = [
        pltpu.make_async_copy(mask, win.at[R:R + T, R:R + T], lsem.at[0]),
        pltpu.make_async_copy(taps, tapv, lsem.at[1]),
        pltpu.make_async_copy(rh_in, rh, lsem.at[2]),
        pltpu.make_async_copy(rl_in, rl, lsem.at[3]),
        pltpu.make_async_copy(th_in, th, lsem.at[4]),
        pltpu.make_async_copy(tl_in, tl, lsem.at[5]),
        pltpu.make_async_copy(target, targ, lsem.at[6]),
    ]
    for load in loads:
        load.start()

    @pl.when(r == 0)
    def _():
        win[:R, :] = jnp.zeros((R, W), F32)

    @pl.when(r == rows - 1)
    def _():
        win[R + T:, :] = jnp.zeros((R, W), F32)

    @pl.when(c == 0)
    def _():
        win[:, :R] = jnp.zeros((W, R), F32)

    @pl.when(c == cols - 1)
    def _():
        win[:, R + T:] = jnp.zeros((W, R), F32)

    barrier = pltpu.get_barrier_semaphore()
    for i in range(4):
        @pl.when(has[i])
        def _(i=i):
            pl.semaphore_signal(barrier, inc=1, device_id=where[i], device_id_type=MESH)
    for d in range(1, 4):
        pl.semaphore_signal(barrier, inc=1, device_id={"kern": peer[d]}, device_id_type=MESH)
    count = 3
    for i in range(4):
        count = count + has[i].astype(jnp.int32)
    pl.semaphore_wait(barrier, count)

    def remote(src, dst, s, d, to):
        return pltpu.make_async_remote_copy(
            src_ref=src, dst_ref=dst, send_sem=s, recv_sem=d, device_id=to, device_id_type=MESH)

    low, mid, high = slice(0, R), slice(R, R + T), slice(R + T, W)
    first, second = slice(R, 2 * R), slice(2 * R, 3 * R)
    halo = [
        (0, mask.at[0:R, :], win.at[high, mid], 1),
        (1, mask.at[R:T, :], win.at[low, mid], 0),
        (2, mask.at[:, 0:R], win.at[mid, high], 3),
        (3, mask.at[:, R:T], win.at[mid, low], 2),
        (2, win.at[low, first], win.at[low, high], 6),
        (2, win.at[high, first], win.at[high, high], 7),
        (3, win.at[low, second], win.at[low, low], 4),
        (3, win.at[high, second], win.at[high, low], 5),
    ]
    copies = [remote(s, d, msend.at[k], mrecv.at[k], where[i]) for i, s, d, k in halo]
    back = (1, 0, 3, 2)

    def on(side, fn):
        pl.when(has[side])(fn)

    for n in range(4):
        on(halo[n][0], copies[n].start)

    for load in loads[1:6]:
        load.wait()
    sign_row = (1 - 2 * (lax.broadcasted_iota(jnp.int32, (1, R), 1) & 1)).astype(F32)
    sign_col = (1 - 2 * (lax.broadcasted_iota(jnp.int32, (R, 1), 0) & 1)).astype(F32)
    taph[...] = jnp.zeros_like(taph)
    for a in range(PARTS):
        taph[a:a + 1, :] = tapv[a // 3, a % 3, T:T + 1, 0:T]
    edge_h, edge_l = split(taph[...])
    rhat[...] = dot3(edge_h, edge_l, rh[:T, :], rl[:T, :])
    for a in range(PARTS):
        corner = tapv[a // 3, a % 3, T:T + 1, T:T + 1]
        for b in range(2):
            at = slice(b * T + R, b * T + T)
            rhat[a:a + 1, at] = rhat[a:a + 1, at] + corner * sign_row

    def tap_spectrum(a, carry):
        part, k = a // 3, lax.rem(a, 3)
        low_h, low_l = split(tapv[part, k, 0:T, 0:T])
        column = tapv[part, k, 0:T, T:T + 1]
        for b in range(2):
            at = slice(b * T, b * T + T)
            value = dot3(low_h, low_l, rh[:T, at], rl[:T, at])
            value = jnp.concatenate([value[:, :R], value[:, R:] + column * sign_row], axis=1)
            vh_, vl_ = split(value)
            xh[:T, at] = vh_
            xl[:T, at] = vl_
        for b in range(2):
            at = slice(b * T, b * T + T)
            value = dot3(th[:, :T], tl[:, :T], xh[:T, at], xl[:T, at])
            edge = sign_col * rhat[pl.ds(a, 1), at]
            for f in range(2):
                block = value[f * T:f * T + T]
                block = jnp.concatenate([block[:R], block[R:] + edge], axis=0)
                for n, x in enumerate(to_complex(block)):
                    hs[a, n, f * R:f * R + R, b * R:b * R + R] = x
        return carry

    lax.fori_loop(0, 3, tap_spectrum, 0)

    loads[0].wait()
    for n in range(2):
        on(back[halo[n][0]], copies[n].wait_recv)
    for n in range(4, 8):
        on(halo[n][0], copies[n].start)

    lax.fori_loop(3, PARTS, tap_spectrum, 0)

    for n in range(2, 8):
        on(back[halo[n][0]], copies[n].wait_recv)

    for half in range(2):
        up = slice(half * T, half * T + T)
        wh_, wl_ = split(win[up, :])
        for b in range(2):
            at = slice(b * T, b * T + T)
            h_, l_ = split(dot3(wh_, wl_, rh[:, at], rl[:, at]))
            xh[up, at] = h_
            xl[up, at] = l_
    for b in range(2):
        at = slice(b * T, b * T + T)
        value = dot3(th[...], tl[...], xh[:, at], xl[:, at])
        for f in range(2):
            for n, x in enumerate(to_complex(value[f * T:f * T + T])):
                ms[n, f * R:f * R + R, b * R:b * R + R] = x

    def inverse_rows(a, carry):
        for b in range(2):
            for f in range(2):
                at = (slice(f * R, f * R + R), slice(b * R, b * R + R))
                m = [ms[n, at[0], at[1]] for n in range(4)]
                h = [hs[a, n, at[0], at[1]] for n in range(4)]
                y = []
                for n in (0, 2):
                    y.append(m[n] * h[n] + m[n + 1] * h[n + 1])
                    y.append(m[n + 1] * h[n] - m[n] * h[n + 1])
                for n, x in enumerate(from_complex(*y)):
                    h_, l_ = split(x)
                    to = (slice(f * T + (n // 2) * R, f * T + (n // 2) * R + R),
                          slice(b * T + (n % 2) * R, b * T + (n % 2) * R + R))
                    xh[to[0], to[1]] = h_
                    xl[to[0], to[1]] = l_
            at = slice(b * T, b * T + T)
            h_, l_ = split(dot3(rh[:T, :], rl[:T, :], xh[:, at], xl[:, at]))
            vh[a, :, at] = h_
            vl[a, :, at] = l_
        return carry

    lax.fori_loop(0, PARTS, inverse_rows, 0)

    def share_rows(q):
        return pl.ds(pl.multiple_of(q * Q, Q), Q)

    def share_amplitude(d):
        at = share_rows(peer[d])
        value = dot3(vh[:, at, :].reshape(PARTS * Q, W), vl[:, at, :].reshape(PARTS * Q, W),
                     th[:, :T], tl[:, :T]).reshape(PARTS, Q, T) * SCALE
        amp[:, at, :] = value
        total = None
        for k in range(3):
            term = weights[k] * (value[k] * value[k] + value[k + 3] * value[k + 3])
            total = term if total is None else total + term
        return total

    sums = []
    for d in range(1, 4):
        ipart[d - 1] = share_amplitude(d)
        copy = remote(ipart.at[d - 1], irecv.at[d - 1], isend.at[d - 1], isem.at[d - 1], {"kern": peer[d]})
        copy.start()
        sums.append(copy)
    total = share_amplitude(0)
    for copy in sums:
        copy.wait_recv()
    intensity = (total + irecv[0] + irecv[1] + irecv[2]) * (1.0 / 12.0)
    own = share_rows(j)
    resv[own, :] = 1.0 / (1.0 + jnp.exp(-8.0 * (intensity - 0.25)))
    shares = []
    for d in range(1, 4):
        copy = remote(resv.at[own, :], resv.at[own, :], asend.at[d - 1], asem.at[d - 1], {"kern": peer[d]})
        copy.start()
        shares.append(copy)

    loads[6].wait()

    def share_product(q):
        at = share_rows(q)
        x = resv[at, :]
        factor = 2.0 * (x - targ[at, :].astype(F32)) * 8.0 * x * (1.0 - x)
        both = [split(factor * (weights[a % 3] * (2.0 / 12.0)) * amp[a, at, :]) for a in range(PARTS)]
        h_ = jnp.concatenate([x[0] for x in both], axis=0)
        l_ = jnp.concatenate([x[1] for x in both], axis=0)
        for b in range(2):
            cut = slice(b * T, b * T + T)
            u, v = split(dot3(h_, l_, rh[:T, cut], rl[:T, cut]).reshape(PARTS, Q, T))
            ph[:, at, cut] = u
            pw[:, at, cut] = v

    share_product(j)
    for d in range(1, 4):
        q = lax.rem(j + 4 - d, 4)
        rows_q = share_rows(q)
        remote(resv.at[rows_q, :], resv.at[rows_q, :], asend.at[d - 1], asem.at[d - 1],
               {"kern": peer[d]}).wait_recv()
        share_product(q)
    store = pltpu.make_async_copy(resv, resist, lsem.at[7])
    store.start()

    windows = []
    for b in range(2):
        at = slice(b * T, b * T + T)
        acc[...] = jnp.zeros_like(acc)

        def gather(a, carry, at=at, b=b):
            value = dot3(th[:, :T], tl[:, :T], ph[a, :, at], pw[a, :, at])
            for f in range(2):
                p = to_complex(value[f * T:f * T + T])
                fr = slice(f * R, f * R + R)
                h = [hs[a, n, fr, b * R:b * R + R] for n in range(4)]
                for n in (0, 2):
                    acc[n, fr, :] += p[n] * h[n] - p[n + 1] * h[n + 1]
                    acc[n + 1, fr, :] += p[n] * h[n + 1] + p[n + 1] * h[n]
            return carry

        lax.fori_loop(0, PARTS, gather, 0)
        for f in range(2):
            fr = slice(f * R, f * R + R)
            for n, x in enumerate(from_complex(*[acc[i, fr, :] for i in range(4)])):
                h_, l_ = split(x)
                to = (slice(f * T + (n // 2) * R, f * T + (n // 2) * R + R),
                      slice(b * T + (n % 2) * R, b * T + (n % 2) * R + R))
                xh[to[0], to[1]] = h_
                xl[to[0], to[1]] = l_
        tsend[b] = dot3(rh[...], rl[...], xh[:, at], xl[:, at]).reshape(8, Q, T)
        for far in range(2):
            for d in range(1, 4):
                chunk = lax.rem(peer[d] + 6, 8) if far == 0 else peer[d] + 2
                n = (b * 2 + far) * 3 + d - 1
                copy = remote(tsend.at[b, chunk], trecv.at[n], tss.at[n], trs.at[n], {"kern": peer[d]})
                copy.start()
                windows.append(copy)

    def summed(b, far):
        n = (b * 2 + far) * 3
        for d in range(3):
            windows[n + d].wait_recv()
        chunk = lax.rem(j + 6, 8) if far == 0 else j + 2
        return tsend[b, chunk] + trecv[n] + trecv[n + 1] + trecv[n + 2]

    down = j < 2
    step = jnp.where(down, 1, -1)
    gives = jnp.logical_or(jnp.logical_and(down, has[1]), jnp.logical_and(jnp.logical_not(down), has[0]))
    takes = jnp.logical_or(jnp.logical_and(down, has[0]), jnp.logical_and(jnp.logical_not(down), has[1]))
    hops = [remote(fsend.at[b], frecv.at[b], fss.at[b], frs.at[b], {"row": r + step}) for b in range(2)]
    near = []
    for b in range(2):
        fsend[b] = summed(b, 0)
        pl.when(gives)(hops[b].start)
        near.append(summed(b, 1))
    for b in range(2):
        gw[:, b * T:b * T + T] = near[b]
    for b in range(2):
        @pl.when(takes)
        def _(b=b):
            hops[b].wait_recv()
            at = slice(b * T, b * T + T)
            gw[:, at] = gw[:, at] + frecv[b]
    g_h, g_l = split(gw[...])
    gw[...] = dot3(g_h, g_l, th[...], tl[...])
    ends = [
        remote(gw.at[:, low], erecv.at[1], ess.at[1], ers.at[1], {"col": c - 1}),
        remote(gw.at[:, high], erecv.at[0], ess.at[0], ers.at[0], {"col": c + 1}),
    ]
    on(2, ends[0].start)
    on(3, ends[1].start)
    lane = lax.broadcasted_iota(jnp.int32, (1, T), 1) // 64
    pixels = jnp.zeros((1, T), F32)
    for k in range(4):
        pixels = jnp.where(lane == k, active[j, k].astype(F32), pixels)
    pixels = pixels * SCALE

    for n, side, cut in ((1, 2, slice(0, R)), (0, 3, slice(R, T))):
        from_cut = slice(cut.start + R, cut.stop + R)

        @pl.when(has[side])
        def _(n=n, side=side, cut=cut, from_cut=from_cut):
            ends[n].wait_recv()
            outv[:, cut] = (gw[:, from_cut] + erecv[side - 2]) * pixels[:, cut]

        @pl.when(jnp.logical_not(has[side]))
        def _(cut=cut, from_cut=from_cut):
            outv[:, cut] = gw[:, from_cut] * pixels[:, cut]

    final = pltpu.make_async_copy(outv, gradient, lsem.at[0])
    final.start()

    for n in range(8):
        on(halo[n][0], copies[n].wait_send)
    for copy in sums + shares + windows:
        copy.wait_send()
    for b in range(2):
        pl.when(gives)(hops[b].wait_send)
    on(2, ends[0].wait_send)
    on(3, ends[1].wait_send)
    store.wait()
    final.wait()


def local(photomask, target_bits, active_blocks, kernel_taps, kernel_weights):
    hbm = pl.BlockSpec(memory_space=pl.ANY)
    smem = pl.BlockSpec(memory_space=pltpu.SMEM)
    vmem = pltpu.VMEM
    dma = pltpu.SemaphoreType.DMA
    scratch = [
        vmem((W, W), F32),
        vmem((2, 3, 2 * R + 1, 2 * R + 1), F32),
        vmem((W, W), BF), vmem((W, W), BF), vmem((W, W), BF), vmem((W, W), BF),
        vmem((T, T), jnp.int32),
        vmem((8, T), F32),
        vmem((8, W), F32),
        vmem((W, W), BF), vmem((W, W), BF),
        vmem((PARTS, 4, T, T), F32),
        vmem((4, T, T), F32),
        vmem((PARTS, T, W), BF), vmem((PARTS, T, W), BF),
        vmem((PARTS, T, T), F32),
        vmem((PARTS, T, W), BF), vmem((PARTS, T, W), BF),
        vmem((3, Q, T), F32), vmem((3, Q, T), F32),
        vmem((T, T), F32),
        vmem((4, T, R), F32),
        vmem((2, 8, Q, T), F32),
        vmem((12, Q, T), F32),
        vmem((2, Q, T), F32), vmem((2, Q, T), F32),
        vmem((Q, W), F32),
        vmem((2, Q, R), F32),
        vmem((Q, T), F32),
        dma((8,)), dma((8,)), dma((8,)),
        dma((3,)), dma((3,)), dma((3,)), dma((3,)),
        dma((12,)), dma((12,)),
        dma((2,)), dma((2,)), dma((2,)), dma((2,)),
    ]
    return pl.pallas_call(
        kernel,
        out_shape=(jax.ShapeDtypeStruct((Q, T), F32), jax.ShapeDtypeStruct((T, T), F32)),
        in_specs=[hbm, hbm, smem, hbm, smem, hbm, hbm, hbm, hbm],
        out_specs=(hbm, hbm),
        scratch_shapes=scratch,
        compiler_params=pltpu.CompilerParams(
            collective_id=0, has_side_effects=True, vmem_limit_bytes=56 * 1024 * 1024),
        name="socs",
    )(photomask, target_bits, active_blocks, kernel_taps, kernel_weights, *[jnp.asarray(t) for t in tables()])


def solution(mesh):
    in_specs = (
        P("row", "col"),
        P("row", "col"),
        P("row", "col"),
        P(None, "kern", None, None),
        P("kern"),
    )
    out_specs = (P(("row", "kern"), "col"), P("row", "col"))
    return jax.shard_map(local, mesh=mesh, in_specs=in_specs, out_specs=out_specs, check_vma=False)
```

time: 460 us -> 68.7 us (0.15)
  the two profiles are of different devices: /device:TPU:8 before, /device:TPU:73 now
where the time goes in v1:
time: 68.7 us; the launch traced here: 68.5 us
  Pallas kernels  61.4 us (89%)
  local copies, waits for them, and re-layouts  6.42 us (9%)
    pallas_call x1, Pallas kernels, local(): pl.pallas_call(kernel, out_shape=(jax.ShapeDtypeStruct((Q, T), F32), jax....  61.4 us
    unnamed x3, local copies, waits for them, and re-layouts  6.42 us

profile of v1, /device:TPU:73, one launch (start us, length us, event | category | flops | bytes accessed | tf_op | source)
XLA Modules:
  0.0 68.5 jit_solution(1954045890961039083)
XLA Ops:
  0.6 3.3 %copy.11.taps = f32[2,3,257,257]{3,2,1,0:T(8,128)} copy(f32[2,3,257,257]{3,0,2,1:T(2,128)} %param.12) | data formatting | bytes 3170352 | tf_op args[3]
  3.9 61.4 %socs.1 = (f32[64,256]{1,0:T(8,128)}, f32[256,256]{1,0:T(8,128)}) custom-call(f32[256,256]{1,0:T(8,128)} %mask.1, s32[256,256]{1,0:T(8,128)} %target.1, s32[4,4]{1,0:T(4,128)} %active.1, f32[2,3,257,257]{3,2,1,0:T(8,128)} %copy.11.taps, f32[3]{0:T(128)} %weights.1, bf16[512,512]{1,0:T(8,128)(2,1)} %constant.8.clone.rh_in, ...), custom_call_target="tpu_custom_call" | custom-call | tf_op jit(solution)/shard_map/socs/pallas_call | solution.py:413
  65.3 1.5 %copy.14 = f32[64,256]{1,0:T(8,128)} copy(f32[64,256]{1,0:T(8,128)} %get-tuple-element.4) | data formatting | bytes 131072
  66.8 1.7 %copy.15 = f32[256,256]{1,0:T(8,128)} copy(f32[256,256]{1,0:T(8,128)} %get-tuple-element.5) | data formatting | bytes 524288

commit v2 on v1

--- a/solution.py
+++ b/solution.py
@@ -54,27 +54,54 @@
     return pr + mr, mi - pi, -(pi + mi), mr - pr
 
 
+def hand_over(gradient, resist, gradient_out, resist_out):
+    gradient_out[...] = gradient[...]
+    resist_out[...] = resist[...]
+
+
+def loop(lo, hi, fn, init):
+    for i in range(lo, hi):
+        fn(i, init)
+
+
 def kernel(
     mask, target, active, taps, weights, rh_in, rl_in, th_in, tl_in,
     gradient, resist,
     win, tapv, rh, rl, th, tl, targ, taph, rhat, xh, xl, hs, ms, vh, vl, amp, ph, pw,
-    ipart, irecv, resv, acc, tsend, trecv, fsend, frecv, gw, erecv, outv,
-    lsem, msend, mrecv, isend, isem, asend, asem, tss, trs, fss, frs, ess, ers,
+    ipart, irecv, resv, acc, tsend, trecv, gw, ecen, eside, outv,
+    lsem, msend, mrecv, psend, precv, isend, isem, asend, asem, tss, trs, ess, ers,
 ):
     r, c, j = lax.axis_index("row"), lax.axis_index("col"), lax.axis_index("kern")
     rows, cols = lax.axis_size("row"), lax.axis_size("col")
-    has = (r > 0, r < rows - 1, c > 0, c < cols - 1)
-    where = ({"row": r - 1}, {"row": r + 1}, {"col": c - 1}, {"col": c + 1})
+    def exists(dr, dc):
+        ok = None
+        for at, d, n in ((r, dr, rows), (c, dc, cols)):
+            if d:
+                one = at > 0 if d < 0 else at < n - 1
+                ok = one if ok is None else jnp.logical_and(ok, one)
+        return ok
+
+    def device(dr, dc):
+        return {"row": r + dr, "col": c + dc}
+
+    around = [(dr, dc) for dr in (-1, 0, 1) for dc in (-1, 0, 1) if dr or dc]
+    down = j < 2
+    step = jnp.where(down, 1, -1)
+    gives = jnp.logical_or(jnp.logical_and(down, r < rows - 1), jnp.logical_and(jnp.logical_not(down), r > 0))
+    takes = jnp.logical_or(jnp.logical_and(down, r > 0), jnp.logical_and(jnp.logical_not(down), r < rows - 1))
     peer = [lax.rem(j + d, 4) for d in range(4)]
 
     loads = [
         pltpu.make_async_copy(mask, win.at[R:R + T, R:R + T], lsem.at[0]),
-        pltpu.make_async_copy(taps, tapv, lsem.at[1]),
-        pltpu.make_async_copy(rh_in, rh, lsem.at[2]),
-        pltpu.make_async_copy(rl_in, rl, lsem.at[3]),
-        pltpu.make_async_copy(th_in, th, lsem.at[4]),
-        pltpu.make_async_copy(tl_in, tl, lsem.at[5]),
-        pltpu.make_async_copy(target, targ, lsem.at[6]),
+        pltpu.make_async_copy(rh_in, rh, lsem.at[1]),
+        pltpu.make_async_copy(rl_in, rl, lsem.at[2]),
+        pltpu.make_async_copy(th_in, th, lsem.at[3]),
+        pltpu.make_async_copy(tl_in, tl, lsem.at[4]),
+        pltpu.make_async_copy(target, targ, lsem.at[5]),
+    ]
+    loads += [
+        pltpu.make_async_copy(taps.at[a % 3, :, a // 3, :], tapv.at[a // 3, a % 3], lsem.at[8 + a])
+        for a in range(PARTS)
     ]
     for load in loads:
         load.start()
@@ -95,16 +122,19 @@
     def _():
         win[:, R + T:] = jnp.zeros((W, R), F32)
 
+    ecen[...] = jnp.zeros_like(ecen)
+    eside[...] = jnp.zeros_like(eside)
     barrier = pltpu.get_barrier_semaphore()
-    for i in range(4):
-        @pl.when(has[i])
-        def _(i=i):
-            pl.semaphore_signal(barrier, inc=1, device_id=where[i], device_id_type=MESH)
+    count = 3
+    for dr, dc in around:
+        ok = exists(dr, dc)
+        count = count + ok.astype(jnp.int32)
+
+        @pl.when(ok)
+        def _(dr=dr, dc=dc):
+            pl.semaphore_signal(barrier, inc=1, device_id=device(dr, dc), device_id_type=MESH)
     for d in range(1, 4):
         pl.semaphore_signal(barrier, inc=1, device_id={"kern": peer[d]}, device_id_type=MESH)
-    count = 3
-    for i in range(4):
-        count = count + has[i].astype(jnp.int32)
     pl.semaphore_wait(barrier, count)
 
     def remote(src, dst, s, d, to):
@@ -112,27 +142,39 @@
             src_ref=src, dst_ref=dst, send_sem=s, recv_sem=d, device_id=to, device_id_type=MESH)
 
     low, mid, high = slice(0, R), slice(R, R + T), slice(R + T, W)
-    first, second = slice(R, 2 * R), slice(2 * R, 3 * R)
-    halo = [
-        (0, mask.at[0:R, :], win.at[high, mid], 1),
-        (1, mask.at[R:T, :], win.at[low, mid], 0),
-        (2, mask.at[:, 0:R], win.at[mid, high], 3),
-        (3, mask.at[:, R:T], win.at[mid, low], 2),
-        (2, win.at[low, first], win.at[low, high], 6),
-        (2, win.at[high, first], win.at[high, high], 7),
-        (3, win.at[low, second], win.at[low, low], 4),
-        (3, win.at[high, second], win.at[high, low], 5),
+    part_rows = R // 4
+
+    def quarter(start, q):
+        return pl.ds(pl.multiple_of(start + q * part_rows, part_rows), part_rows)
+
+    pieces = [
+        (-1, 0, mask.at[quarter(0, j), :], win.at[quarter(R + T, j), mid]),
+        (1, 0, mask.at[quarter(R, j), :], win.at[quarter(0, j), mid]),
+        (0, -1, mask.at[:, 0:R], win.at[mid, high]),
+        (0, 1, mask.at[:, R:T], win.at[mid, low]),
+        (-1, -1, mask.at[0:R, 0:R], win.at[high, high]),
+        (-1, 1, mask.at[0:R, R:T], win.at[high, low]),
+        (1, -1, mask.at[R:T, 0:R], win.at[low, high]),
+        (1, 1, mask.at[R:T, R:T], win.at[low, low]),
     ]
-    copies = [remote(s, d, msend.at[k], mrecv.at[k], where[i]) for i, s, d, k in halo]
-    back = (1, 0, 3, 2)
-
-    def on(side, fn):
-        pl.when(has[side])(fn)
-
-    for n in range(4):
-        on(halo[n][0], copies[n].start)
-
-    for load in loads[1:6]:
+    copies = [remote(src, dst, msend.at[n], mrecv.at[n], device(dr, dc))
+              for n, (dr, dc, src, dst) in enumerate(pieces)]
+    for n in range(8):
+        pl.when(exists(*pieces[n][:2]))(copies[n].start)
+
+    def arrived(n):
+        pl.when(exists(-pieces[n][0], -pieces[n][1]))(copies[n].wait_recv)
+
+    def passed(d):
+        return [
+            remote(win.at[quarter(start, j), mid], win.at[quarter(start, j), mid],
+                   psend.at[2 * d - 2 + n], precv.at[2 * d - 2 + n], {"kern": peer[d]})
+            for n, start in enumerate((R + T, 0))
+        ]
+
+    passes = [passed(d) for d in range(1, 4)]
+
+    for load in loads[1:5] + loads[6:]:
         load.wait()
     sign_row = (1 - 2 * (lax.broadcasted_iota(jnp.int32, (1, R), 1) & 1)).astype(F32)
     sign_col = (1 - 2 * (lax.broadcasted_iota(jnp.int32, (R, 1), 0) & 1)).astype(F32)
@@ -148,7 +190,7 @@
             rhat[a:a + 1, at] = rhat[a:a + 1, at] + corner * sign_row
 
     def tap_spectrum(a, carry):
-        part, k = a // 3, lax.rem(a, 3)
+        part, k = a // 3, a % 3
         low_h, low_l = split(tapv[part, k, 0:T, 0:T])
         column = tapv[part, k, 0:T, T:T + 1]
         for b in range(2):
@@ -161,7 +203,7 @@
         for b in range(2):
             at = slice(b * T, b * T + T)
             value = dot3(th[:, :T], tl[:, :T], xh[:T, at], xl[:T, at])
-            edge = sign_col * rhat[pl.ds(a, 1), at]
+            edge = sign_col * rhat[a:a + 1, at]
             for f in range(2):
                 block = value[f * T:f * T + T]
                 block = jnp.concatenate([block[:R], block[R:] + edge], axis=0)
@@ -169,18 +211,24 @@
                     hs[a, n, f * R:f * R + R, b * R:b * R + R] = x
         return carry
 
-    lax.fori_loop(0, 3, tap_spectrum, 0)
+    loop(0, 4, tap_spectrum, 0)
+
+    for n in range(2):
+        arrived(n)
+        for d in range(3):
+            pl.when(exists(-pieces[n][0], 0))(passes[d][n].start)
+
+    loop(4, PARTS, tap_spectrum, 0)
 
     loads[0].wait()
-    for n in range(2):
-        on(back[halo[n][0]], copies[n].wait_recv)
-    for n in range(4, 8):
-        on(halo[n][0], copies[n].start)
-
-    lax.fori_loop(3, PARTS, tap_spectrum, 0)
-
     for n in range(2, 8):
-        on(back[halo[n][0]], copies[n].wait_recv)
+        arrived(n)
+    for d in range(1, 4):
+        q = lax.rem(j + 4 - d, 4)
+        for n, start in enumerate((R + T, 0)):
+            at = win.at[quarter(start, q), mid]
+            came = remote(at, at, psend.at[2 * d - 2 + n], precv.at[2 * d - 2 + n], {"kern": peer[d]})
+            pl.when(exists(-pieces[n][0], 0))(came.wait_recv)
 
     for half in range(2):
         up = slice(half * T, half * T + T)
@@ -219,7 +267,7 @@
             vl[a, :, at] = l_
         return carry
 
-    lax.fori_loop(0, PARTS, inverse_rows, 0)
+    loop(0, PARTS, inverse_rows, 0)
 
     def share_rows(q):
         return pl.ds(pl.multiple_of(q * Q, Q), Q)
@@ -253,7 +301,7 @@
         copy.start()
         shares.append(copy)
 
-    loads[6].wait()
+    loads[5].wait()
 
     def share_product(q):
         at = share_rows(q)
@@ -294,7 +342,7 @@
                     acc[n + 1, fr, :] += p[n] * h[n + 1] + p[n + 1] * h[n]
             return carry
 
-        lax.fori_loop(0, PARTS, gather, 0)
+        loop(0, PARTS, gather, 0)
         for f in range(2):
             fr = slice(f * R, f * R + R)
             for n, x in enumerate(from_complex(*[acc[i, fr, :] for i in range(4)])):
@@ -312,68 +360,50 @@
                 copy.start()
                 windows.append(copy)
 
-    def summed(b, far):
-        n = (b * 2 + far) * 3
-        for d in range(3):
-            windows[n + d].wait_recv()
-        chunk = lax.rem(j + 6, 8) if far == 0 else j + 2
-        return tsend[b, chunk] + trecv[n] + trecv[n + 1] + trecv[n + 2]
-
-    down = j < 2
-    step = jnp.where(down, 1, -1)
-    gives = jnp.logical_or(jnp.logical_and(down, has[1]), jnp.logical_and(jnp.logical_not(down), has[0]))
-    takes = jnp.logical_or(jnp.logical_and(down, has[0]), jnp.logical_and(jnp.logical_not(down), has[1]))
-    hops = [remote(fsend.at[b], frecv.at[b], fss.at[b], frs.at[b], {"row": r + step}) for b in range(2)]
-    near = []
-    for b in range(2):
-        fsend[b] = summed(b, 0)
-        pl.when(gives)(hops[b].start)
-        near.append(summed(b, 1))
-    for b in range(2):
-        gw[:, b * T:b * T + T] = near[b]
-    for b in range(2):
-        @pl.when(takes)
-        def _(b=b):
-            hops[b].wait_recv()
-            at = slice(b * T, b * T + T)
-            gw[:, at] = gw[:, at] + frecv[b]
+    for far in range(2):
+        for b in range(2):
+            n = (b * 2 + far) * 3
+            for d in range(3):
+                windows[n + d].wait_recv()
+            chunk = lax.rem(j + 6, 8) if far == 0 else j + 2
+            gw[far * Q:far * Q + Q, b * T:b * T + T] = tsend[b, chunk] + trecv[n] + trecv[n + 1] + trecv[n + 2]
     g_h, g_l = split(gw[...])
     gw[...] = dot3(g_h, g_l, th[...], tl[...])
+    far_rows, near_rows = slice(0, Q), slice(Q, 2 * Q)
+    west, east = exists(0, -1), exists(0, 1)
     ends = [
-        remote(gw.at[:, low], erecv.at[1], ess.at[1], ers.at[1], {"col": c - 1}),
-        remote(gw.at[:, high], erecv.at[0], ess.at[0], ers.at[0], {"col": c + 1}),
+        (gives, takes, gw.at[far_rows, mid], ecen, device(step, 0)),
+        (jnp.logical_and(gives, west), jnp.logical_and(takes, east), gw.at[far_rows, low], eside.at[0], device(step, -1)),
+        (jnp.logical_and(gives, east), jnp.logical_and(takes, west), gw.at[far_rows, high], eside.at[1], device(step, 1)),
+        (west, east, gw.at[near_rows, low], eside.at[2], device(0, -1)),
+        (east, west, gw.at[near_rows, high], eside.at[3], device(0, 1)),
     ]
-    on(2, ends[0].start)
-    on(3, ends[1].start)
+    hops = [remote(src, dst, ess.at[n], ers.at[n], to) for n, (_, _, src, dst, to) in enumerate(ends)]
+    for n in range(5):
+        pl.when(ends[n][0])(hops[n].start)
     lane = lax.broadcasted_iota(jnp.int32, (1, T), 1) // 64
     pixels = jnp.zeros((1, T), F32)
     for k in range(4):
         pixels = jnp.where(lane == k, active[j, k].astype(F32), pixels)
     pixels = pixels * SCALE
-
-    for n, side, cut in ((1, 2, slice(0, R)), (0, 3, slice(R, T))):
-        from_cut = slice(cut.start + R, cut.stop + R)
-
-        @pl.when(has[side])
-        def _(n=n, side=side, cut=cut, from_cut=from_cut):
-            ends[n].wait_recv()
-            outv[:, cut] = (gw[:, from_cut] + erecv[side - 2]) * pixels[:, cut]
-
-        @pl.when(jnp.logical_not(has[side]))
-        def _(cut=cut, from_cut=from_cut):
-            outv[:, cut] = gw[:, from_cut] * pixels[:, cut]
+    for n in range(5):
+        pl.when(ends[n][1])(hops[n].wait_recv)
+    own_part = gw[near_rows, mid] + ecen[...]
+    outv[:, :R] = (own_part[:, :R] + eside[1] + eside[3]) * pixels[:, :R]
+    outv[:, R:] = (own_part[:, R:] + eside[0] + eside[2]) * pixels[:, R:]
 
     final = pltpu.make_async_copy(outv, gradient, lsem.at[0])
     final.start()
 
     for n in range(8):
-        on(halo[n][0], copies[n].wait_send)
+        pl.when(exists(*pieces[n][:2]))(copies[n].wait_send)
+    for n in range(2):
+        for d in range(3):
+            pl.when(exists(-pieces[n][0], 0))(passes[d][n].wait_send)
     for copy in sums + shares + windows:
         copy.wait_send()
-    for b in range(2):
-        pl.when(gives)(hops[b].wait_send)
-    on(2, ends[0].wait_send)
-    on(3, ends[1].wait_send)
+    for n in range(5):
+        pl.when(ends[n][0])(hops[n].wait_send)
     store.wait()
     final.wait()
 
@@ -401,25 +431,28 @@
         vmem((4, T, R), F32),
         vmem((2, 8, Q, T), F32),
         vmem((12, Q, T), F32),
-        vmem((2, Q, T), F32), vmem((2, Q, T), F32),
-        vmem((Q, W), F32),
-        vmem((2, Q, R), F32),
+        vmem((2 * Q, W), F32),
+        vmem((Q, T), F32), vmem((4, Q, R), F32),
         vmem((Q, T), F32),
-        dma((8,)), dma((8,)), dma((8,)),
+        dma((14,)), dma((8,)), dma((8,)),
+        dma((6,)), dma((6,)),
         dma((3,)), dma((3,)), dma((3,)), dma((3,)),
         dma((12,)), dma((12,)),
-        dma((2,)), dma((2,)), dma((2,)), dma((2,)),
+        dma((5,)), dma((5,)),
     ]
-    return pl.pallas_call(
+    outs = (jax.ShapeDtypeStruct((Q, T), F32), jax.ShapeDtypeStruct((T, T), F32))
+    gradient, resist = pl.pallas_call(
         kernel,
-        out_shape=(jax.ShapeDtypeStruct((Q, T), F32), jax.ShapeDtypeStruct((T, T), F32)),
+        out_shape=outs,
         in_specs=[hbm, hbm, smem, hbm, smem, hbm, hbm, hbm, hbm],
         out_specs=(hbm, hbm),
         scratch_shapes=scratch,
         compiler_params=pltpu.CompilerParams(
             collective_id=0, has_side_effects=True, vmem_limit_bytes=56 * 1024 * 1024),
         name="socs",
-    )(photomask, target_bits, active_blocks, kernel_taps, kernel_weights, *[jnp.asarray(t) for t in tables()])
+    )(photomask, target_bits, active_blocks, kernel_taps.transpose(1, 2, 0, 3), kernel_weights,
+      *[jnp.asarray(t) for t in tables()])
+    return pl.pallas_call(hand_over, out_shape=outs, name="hand_over")(gradient, resist)
 
 
 def solution(mesh):

time: 68.7 us -> 61.5 us (0.90)
  the two profiles are of different devices: /device:TPU:73 before, /device:TPU:25 now
where the time goes in v2:
time: 61.5 us; the launch traced here: 61.3 us
  Pallas kernels  60.7 us (99%)
  between operations  0.64 us (1%)
    pallas_call x1, Pallas kernels, local(): pl.pallas_call(kernel, out_shape=outs, in_specs=[hbm, hbm, smem, hbm, sme...  59 us
    pallas_call x1, Pallas kernels, local(): pl.pallas_call(hand_over, out_shape=outs, name='hand_over')  1.72 us

profile of v2, /device:TPU:25, one launch (start us, length us, event | category | flops | bytes accessed | tf_op | source)
XLA Modules:
  0.0 61.3 jit_solution(3627555017568084645)
XLA Ops:
  0.6 59.0 %socs.1 = (f32[64,256]{1,0:T(8,128)}, f32[256,256]{1,0:T(8,128)}) custom-call(f32[256,256]{1,0:T(8,128)} %mask.1, s32[256,256]{1,0:T(8,128)} %target.1, s32[4,4]{1,0:T(4,128)} %active.1, f32[3,257,2,257]{3,2,1,0:T(2,128)} %bitcast.1, f32[3]{0:T(128)} %weights.1, bf16[512,512]{1,0:T(8,128)(2,1)} %constant.8.clone.rh_in, ...), custom_call_target="tpu_custom_call" | custom-call | tf_op jit(solution)/shard_map/socs/pallas_call | solution.py:444
  59.6 1.7 %hand_over.1 = (f32[64,256]{1,0:T(8,128)}, f32[256,256]{1,0:T(8,128)}) custom-call(f32[64,256]{1,0:T(8,128)} %get-tuple-element.4.gradient, f32[256,256]{1,0:T(8,128)} %get-tuple-element.5.resist), custom_call_target="tpu_custom_call" | custom-call | tf_op jit(solution)/shard_map/hand_over/pallas_call | solution.py:455

commit v3 on v2

--- a/solution.py
+++ b/solution.py
@@ -54,9 +54,15 @@
     return pr + mr, mi - pi, -(pi + mi), mr - pr
 
 
-def hand_over(gradient, resist, gradient_out, resist_out):
-    gradient_out[...] = gradient[...]
-    resist_out[...] = resist[...]
+def hand_over(gradient, resist, gradient_out, resist_out, sems):
+    copies = [
+        pltpu.make_async_copy(resist, resist_out, sems.at[0]),
+        pltpu.make_async_copy(gradient, gradient_out, sems.at[1]),
+    ]
+    for copy in copies:
+        copy.start()
+    for copy in copies:
+        copy.wait()
 
 
 def loop(lo, hi, fn, init):
@@ -67,9 +73,9 @@
 def kernel(
     mask, target, active, taps, weights, rh_in, rl_in, th_in, tl_in,
     gradient, resist,
-    win, tapv, rh, rl, th, tl, targ, taph, rhat, xh, xl, hs, ms, vh, vl, amp, ph, pw,
-    ipart, irecv, resv, acc, tsend, trecv, gw, ecen, eside, outv,
-    lsem, msend, mrecv, psend, precv, isend, isem, asend, asem, tss, trs, ess, ers,
+    win, tapv, rh, rl, th, tl, targ, taph, rhat, xh, xl, mpart, hs, ms, vh, vl, amp, ph, pw,
+    ipart, ione, imid, itwo, resv, acc, tsend, tone, tmid, ttwo, gw, ecen, eside, outv,
+    lsem, msend, mrecv, psend, precv, isend, isem, asend, asem, tss, trs, uss, urs, ess, ers,
 ):
     r, c, j = lax.axis_index("row"), lax.axis_index("col"), lax.axis_index("kern")
     rows, cols = lax.axis_size("row"), lax.axis_size("col")
@@ -91,6 +97,19 @@
     takes = jnp.logical_or(jnp.logical_and(down, r > 0), jnp.logical_and(jnp.logical_not(down), r < rows - 1))
     peer = [lax.rem(j + d, 4) for d in range(4)]
 
+    ecen[...] = jnp.zeros_like(ecen)
+    eside[...] = jnp.zeros_like(eside)
+    barrier = pltpu.get_barrier_semaphore()
+    count = 3
+    for dr, dc in around:
+        ok = exists(dr, dc)
+        count = count + ok.astype(jnp.int32)
+
+        @pl.when(ok)
+        def _(dr=dr, dc=dc):
+            pl.semaphore_signal(barrier, inc=1, device_id=device(dr, dc), device_id_type=MESH)
+    for d in range(1, 4):
+        pl.semaphore_signal(barrier, inc=1, device_id={"kern": peer[d]}, device_id_type=MESH)
     loads = [
         pltpu.make_async_copy(mask, win.at[R:R + T, R:R + T], lsem.at[0]),
         pltpu.make_async_copy(rh_in, rh, lsem.at[1]),
@@ -122,19 +141,6 @@
     def _():
         win[:, R + T:] = jnp.zeros((W, R), F32)
 
-    ecen[...] = jnp.zeros_like(ecen)
-    eside[...] = jnp.zeros_like(eside)
-    barrier = pltpu.get_barrier_semaphore()
-    count = 3
-    for dr, dc in around:
-        ok = exists(dr, dc)
-        count = count + ok.astype(jnp.int32)
-
-        @pl.when(ok)
-        def _(dr=dr, dc=dc):
-            pl.semaphore_signal(barrier, inc=1, device_id=device(dr, dc), device_id_type=MESH)
-    for d in range(1, 4):
-        pl.semaphore_signal(barrier, inc=1, device_id={"kern": peer[d]}, device_id_type=MESH)
     pl.semaphore_wait(barrier, count)
 
     def remote(src, dst, s, d, to):
@@ -221,7 +227,17 @@
     loop(4, PARTS, tap_spectrum, 0)
 
     loads[0].wait()
-    for n in range(2, 8):
+    for n in (2, 3):
+        arrived(n)
+
+    def mask_columns(values):
+        h_, l_ = split(values)
+        return [split(dot3(h_, l_, rh[:, b * T:b * T + T], rl[:, b * T:b * T + T])) for b in range(2)]
+
+    for b, (h_, l_) in enumerate(mask_columns(win[mid, :])):
+        mpart[:, b * T:b * T + T] = dot3(th[:, mid], tl[:, mid], h_, l_)
+
+    for n in range(4, 8):
         arrived(n)
     for d in range(1, 4):
         q = lax.rem(j + 4 - d, 4)
@@ -230,17 +246,9 @@
             came = remote(at, at, psend.at[2 * d - 2 + n], precv.at[2 * d - 2 + n], {"kern": peer[d]})
             pl.when(exists(-pieces[n][0], 0))(came.wait_recv)
 
-    for half in range(2):
-        up = slice(half * T, half * T + T)
-        wh_, wl_ = split(win[up, :])
-        for b in range(2):
-            at = slice(b * T, b * T + T)
-            h_, l_ = split(dot3(wh_, wl_, rh[:, at], rl[:, at]))
-            xh[up, at] = h_
-            xl[up, at] = l_
-    for b in range(2):
-        at = slice(b * T, b * T + T)
-        value = dot3(th[...], tl[...], xh[:, at], xl[:, at])
+    outer = [jnp.concatenate([t[:, low], t[:, high]], axis=1) for t in (th, tl)]
+    for b, (h_, l_) in enumerate(mask_columns(jnp.concatenate([win[low, :], win[high, :]], axis=0))):
+        value = mpart[:, b * T:b * T + T] + dot3(*outer, h_, l_)
         for f in range(2):
             for n, x in enumerate(to_complex(value[f * T:f * T + T])):
                 ms[n, f * R:f * R + R, b * R:b * R + R] = x
@@ -269,11 +277,15 @@
 
     loop(0, PARTS, inverse_rows, 0)
 
-    def share_rows(q):
-        return pl.ds(pl.multiple_of(q * Q, Q), Q)
-
-    def share_amplitude(d):
-        at = share_rows(peer[d])
+    def partner(kind, at):
+        return at + 1 - 2 * lax.rem(at, 2) if kind == 0 else 3 - at
+
+    pair = (partner(0, j), partner(1, j))
+    def rows_of(i):
+        return slice(i * Q, i * Q + Q)
+
+    def amplitudes(i):
+        at = rows_of(i)
         value = dot3(vh[:, at, :].reshape(PARTS * Q, W), vl[:, at, :].reshape(PARTS * Q, W),
                      th[:, :T], tl[:, :T]).reshape(PARTS, Q, T) * SCALE
         amp[:, at, :] = value
@@ -283,29 +295,33 @@
             total = term if total is None else total + term
         return total
 
+    halves = (slice(0, R), slice(R, T))
     sums = []
-    for d in range(1, 4):
-        ipart[d - 1] = share_amplitude(d)
-        copy = remote(ipart.at[d - 1], irecv.at[d - 1], isend.at[d - 1], isem.at[d - 1], {"kern": peer[d]})
-        copy.start()
-        sums.append(copy)
-    total = share_amplitude(0)
-    for copy in sums:
-        copy.wait_recv()
-    intensity = (total + irecv[0] + irecv[1] + irecv[2]) * (1.0 / 12.0)
-    own = share_rows(j)
-    resv[own, :] = 1.0 / (1.0 + jnp.exp(-8.0 * (intensity - 0.25)))
+    for i in range(4):
+        ipart[i] = amplitudes(i)
+        for half in range(2):
+            n = 2 * i + half
+            copy = remote(ipart.at[i, :, halves[half]], ione.at[n], isend.at[n], isem.at[n], {"kern": pair[half]})
+            copy.start()
+            sums.append(copy)
     shares = []
-    for d in range(1, 4):
-        copy = remote(resv.at[own, :], resv.at[own, :], asend.at[d - 1], asem.at[d - 1], {"kern": peer[d]})
-        copy.start()
-        shares.append(copy)
+    for i in range(4):
+        for half in range(2):
+            n = 2 * i + half
+            sums[n].wait_recv()
+            imid[n] = ipart[i, :, halves[half]] + ione[n]
+            copy = remote(imid.at[n], itwo.at[n], asend.at[n], asem.at[n], {"kern": pair[1 - half]})
+            copy.start()
+            shares.append(copy)
 
     loads[5].wait()
-
-    def share_product(q):
-        at = share_rows(q)
-        x = resv[at, :]
+    for i in range(4):
+        at = rows_of(i)
+        for half in range(2):
+            shares[2 * i + half].wait_recv()
+        intensity = jnp.concatenate([imid[2 * i] + itwo[2 * i], imid[2 * i + 1] + itwo[2 * i + 1]], axis=1) * (1.0 / 12.0)
+        x = 1.0 / (1.0 + jnp.exp(-8.0 * (intensity - 0.25)))
+        resv[at, :] = x
         factor = 2.0 * (x - targ[at, :].astype(F32)) * 8.0 * x * (1.0 - x)
         both = [split(factor * (weights[a % 3] * (2.0 / 12.0)) * amp[a, at, :]) for a in range(PARTS)]
         h_ = jnp.concatenate([x[0] for x in both], axis=0)
@@ -315,18 +331,10 @@
             u, v = split(dot3(h_, l_, rh[:T, cut], rl[:T, cut]).reshape(PARTS, Q, T))
             ph[:, at, cut] = u
             pw[:, at, cut] = v
-
-    share_product(j)
-    for d in range(1, 4):
-        q = lax.rem(j + 4 - d, 4)
-        rows_q = share_rows(q)
-        remote(resv.at[rows_q, :], resv.at[rows_q, :], asend.at[d - 1], asem.at[d - 1],
-               {"kern": peer[d]}).wait_recv()
-        share_product(q)
     store = pltpu.make_async_copy(resv, resist, lsem.at[7])
     store.start()
 
-    windows = []
+    firsts = []
     for b in range(2):
         at = slice(b * T, b * T + T)
         acc[...] = jnp.zeros_like(acc)
@@ -351,22 +359,38 @@
                       slice(b * T + (n % 2) * R, b * T + (n % 2) * R + R))
                 xh[to[0], to[1]] = h_
                 xl[to[0], to[1]] = l_
-        tsend[b] = dot3(rh[...], rl[...], xh[:, at], xl[:, at]).reshape(8, Q, T)
-        for far in range(2):
-            for d in range(1, 4):
-                chunk = lax.rem(peer[d] + 6, 8) if far == 0 else peer[d] + 2
-                n = (b * 2 + far) * 3 + d - 1
-                copy = remote(tsend.at[b, chunk], trecv.at[n], tss.at[n], trs.at[n], {"kern": peer[d]})
+        value = dot3(rh[...], rl[...], xh[:, at], xl[:, at])
+        for q in range(4):
+            for far in range(2):
+                m = (q + 6) % 8 if far == 0 else q + 2
+                tsend[b, q, far] = value[m * Q:m * Q + Q]
+        for half in range(2):
+            to = pair[half]
+            for slot, owner in enumerate((to, partner(1 - half, to))):
+                n = (b * 2 + half) * 2 + slot
+                copy = remote(tsend.at[b, owner, :, :, half * R:half * R + R], tone.at[n],
+                              tss.at[n], trs.at[n], {"kern": to})
                 copy.start()
-                windows.append(copy)
-
-    for far in range(2):
-        for b in range(2):
-            n = (b * 2 + far) * 3
-            for d in range(3):
-                windows[n + d].wait_recv()
-            chunk = lax.rem(j + 6, 8) if far == 0 else j + 2
-            gw[far * Q:far * Q + Q, b * T:b * T + T] = tsend[b, chunk] + trecv[n] + trecv[n + 1] + trecv[n + 2]
+                firsts.append(copy)
+
+    seconds = []
+    for b in range(2):
+        for half in range(2):
+            n = b * 2 + half
+            firsts[2 * n].wait_recv()
+            firsts[2 * n + 1].wait_recv()
+            to = pair[1 - half]
+            tmid[n] = tsend[b, to, :, :, half * R:half * R + R] + tone[2 * n + 1]
+            copy = remote(tmid.at[n], ttwo.at[n], uss.at[n], urs.at[n], {"kern": to})
+            copy.start()
+            seconds.append(copy)
+
+    for b in range(2):
+        for half in range(2):
+            n = b * 2 + half
+            seconds[n].wait_recv()
+            part = tsend[b, j, :, :, half * R:half * R + R] + tone[2 * n] + ttwo[n]
+            gw[:, b * T + half * R:b * T + half * R + R] = part.reshape(2 * Q, R)
     g_h, g_l = split(gw[...])
     gw[...] = dot3(g_h, g_l, th[...], tl[...])
     far_rows, near_rows = slice(0, Q), slice(Q, 2 * Q)
@@ -400,7 +424,7 @@
     for n in range(2):
         for d in range(3):
             pl.when(exists(-pieces[n][0], 0))(passes[d][n].wait_send)
-    for copy in sums + shares + windows:
+    for copy in sums + shares + firsts + seconds:
         copy.wait_send()
     for n in range(5):
         pl.when(ends[n][0])(hops[n].wait_send)
@@ -421,23 +445,24 @@
         vmem((8, T), F32),
         vmem((8, W), F32),
         vmem((W, W), BF), vmem((W, W), BF),
+        vmem((W, W), F32),
         vmem((PARTS, 4, T, T), F32),
         vmem((4, T, T), F32),
         vmem((PARTS, T, W), BF), vmem((PARTS, T, W), BF),
         vmem((PARTS, T, T), F32),
         vmem((PARTS, T, W), BF), vmem((PARTS, T, W), BF),
-        vmem((3, Q, T), F32), vmem((3, Q, T), F32),
+        vmem((4, Q, T), F32), vmem((8, Q, R), F32), vmem((8, Q, R), F32), vmem((8, Q, R), F32),
         vmem((T, T), F32),
         vmem((4, T, R), F32),
-        vmem((2, 8, Q, T), F32),
-        vmem((12, Q, T), F32),
+        vmem((2, 4, 2, Q, T), F32),
+        vmem((8, 2, Q, R), F32), vmem((4, 2, Q, R), F32), vmem((4, 2, Q, R), F32),
         vmem((2 * Q, W), F32),
         vmem((Q, T), F32), vmem((4, Q, R), F32),
         vmem((Q, T), F32),
         dma((14,)), dma((8,)), dma((8,)),
         dma((6,)), dma((6,)),
-        dma((3,)), dma((3,)), dma((3,)), dma((3,)),
-        dma((12,)), dma((12,)),
+        dma((8,)), dma((8,)), dma((8,)), dma((8,)),
+        dma((8,)), dma((8,)), dma((4,)), dma((4,)),
         dma((5,)), dma((5,)),
     ]
     outs = (jax.ShapeDtypeStruct((Q, T), F32), jax.ShapeDtypeStruct((T, T), F32))
@@ -452,7 +477,9 @@
         name="socs",
     )(photomask, target_bits, active_blocks, kernel_taps.transpose(1, 2, 0, 3), kernel_weights,
       *[jnp.asarray(t) for t in tables()])
-    return pl.pallas_call(hand_over, out_shape=outs, name="hand_over")(gradient, resist)
+    return pl.pallas_call(
+        hand_over, out_shape=outs, in_specs=[hbm, hbm], out_specs=(hbm, hbm), scratch_shapes=[dma((2,))],
+        name="hand_over")(gradient, resist)
 
 
 def solution(mesh):

time: 61.5 us -> 65 us (1.057)
  Pallas kernels: 60.7 us -> 64.1 us
    pallas_call x1, Pallas kernels: 1.72 us -> 11 us  [local(): pl.pallas_call(hand_over, out_shape=outs, in_specs=[hbm, hbm], out_specs=...]
    pallas_call x1, Pallas kernels: 59 us -> 53.1 us  [local(): pl.pallas_call(kernel, out_shape=outs, in_specs=[hbm, hbm, smem, hbm, sme...]
where the time goes in v3:
time: 65 us; the launch traced here: 64.9 us
  Pallas kernels  64.1 us (99%)
  between operations  0.8 us (1%)
    pallas_call x1, Pallas kernels, local(): pl.pallas_call(kernel, out_shape=outs, in_specs=[hbm, hbm, smem, hbm, sme...  53.1 us
    pallas_call x1, Pallas kernels, local(): pl.pallas_call(hand_over, out_shape=outs, in_specs=[hbm, hbm], out_specs=...  11 us

profile of v3, /device:TPU:25, one launch (start us, length us, event | category | flops | bytes accessed | tf_op | source)
XLA Modules:
  0.0 64.9 jit_solution(7184691996815370121)
XLA Ops:
  0.6 53.1 %socs.1 = (f32[64,256]{1,0:T(8,128)}, f32[256,256]{1,0:T(8,128)}) custom-call(f32[256,256]{1,0:T(8,128)} %mask.1, s32[256,256]{1,0:T(8,128)} %target.1, s32[4,4]{1,0:T(4,128)} %active.1, f32[3,257,2,257]{3,2,1,0:T(2,128)} %bitcast.1, f32[3]{0:T(128)} %weights.1, bf16[512,512]{1,0:T(8,128)(2,1)} %constant.8.clone.rh_in, ...), custom_call_target="tpu_custom_call" | custom-call | tf_op jit(solution)/shard_map/socs/pallas_call | solution.py:469
  53.7 11.0 %hand_over.1 = (f32[64,256]{1,0:T(8,128)}, f32[256,256]{1,0:T(8,128)}) custom-call(f32[64,256]{1,0:T(8,128)} %get-tuple-element.4.gradient, f32[256,256]{1,0:T(8,128)} %get-tuple-element.5.resist), custom_call_target="tpu_custom_call" | custom-call | tf_op jit(solution)/shard_map/hand_over/pallas_call | solution.py:480

commit v4 on v3

--- a/solution.py
+++ b/solution.py
@@ -54,15 +54,9 @@
     return pr + mr, mi - pi, -(pi + mi), mr - pr
 
 
-def hand_over(gradient, resist, gradient_out, resist_out, sems):
-    copies = [
-        pltpu.make_async_copy(resist, resist_out, sems.at[0]),
-        pltpu.make_async_copy(gradient, gradient_out, sems.at[1]),
-    ]
-    for copy in copies:
-        copy.start()
-    for copy in copies:
-        copy.wait()
+def hand_over(gradient, resist, gradient_out, resist_out):
+    gradient_out[...] = gradient[...]
+    resist_out[...] = resist[...]
 
 
 def loop(lo, hi, fn, init):
@@ -477,9 +471,7 @@
         name="socs",
     )(photomask, target_bits, active_blocks, kernel_taps.transpose(1, 2, 0, 3), kernel_weights,
       *[jnp.asarray(t) for t in tables()])
-    return pl.pallas_call(
-        hand_over, out_shape=outs, in_specs=[hbm, hbm], out_specs=(hbm, hbm), scratch_shapes=[dma((2,))],
-        name="hand_over")(gradient, resist)
+    return pl.pallas_call(hand_over, out_shape=outs, name="hand_over")(gradient, resist)
 
 
 def solution(mesh):

time: 65 us -> 55.6 us (0.86)
  Pallas kernels: 64.1 us -> 54.8 us
    pallas_call x1, Pallas kernels: 11 us -> 1.72 us  [local(): pl.pallas_call(hand_over, out_shape=outs, name='hand_over')]
where the time goes in v4:
time: 55.6 us; the launch traced here: 55.4 us
  Pallas kernels  54.8 us (99%)
  between operations  0.64 us (1%)
    pallas_call x1, Pallas kernels, local(): pl.pallas_call(kernel, out_shape=outs, in_specs=[hbm, hbm, smem, hbm, sme...  53.1 us
    pallas_call x1, Pallas kernels, local(): pl.pallas_call(hand_over, out_shape=outs, name='hand_over')  1.72 us

profile of v4, /device:TPU:25, one launch (start us, length us, event | category | flops | bytes accessed | tf_op | source)
XLA Modules:
  0.0 55.4 jit_solution(12152228307204644141)
XLA Ops:
  0.6 53.1 %socs.1 = (f32[64,256]{1,0:T(8,128)}, f32[256,256]{1,0:T(8,128)}) custom-call(f32[256,256]{1,0:T(8,128)} %mask.1, s32[256,256]{1,0:T(8,128)} %target.1, s32[4,4]{1,0:T(4,128)} %active.1, f32[3,257,2,257]{3,2,1,0:T(2,128)} %bitcast.1, f32[3]{0:T(128)} %weights.1, bf16[512,512]{1,0:T(8,128)(2,1)} %constant.8.clone.rh_in, ...), custom_call_target="tpu_custom_call" | custom-call | tf_op jit(solution)/shard_map/socs/pallas_call | solution.py:463
  53.7 1.7 %hand_over.1 = (f32[64,256]{1,0:T(8,128)}, f32[256,256]{1,0:T(8,128)}) custom-call(f32[64,256]{1,0:T(8,128)} %get-tuple-element.4.gradient, f32[256,256]{1,0:T(8,128)} %get-tuple-element.5.resist), custom_call_target="tpu_custom_call" | custom-call | tf_op jit(solution)/shard_map/hand_over/pallas_call | solution.py:474

commit v5 on v4

--- a/solution.py
+++ b/solution.py
@@ -54,21 +54,23 @@
     return pr + mr, mi - pi, -(pi + mi), mr - pr
 
 
-def hand_over(gradient, resist, gradient_out, resist_out):
-    gradient_out[...] = gradient[...]
-    resist_out[...] = resist[...]
-
-
 def loop(lo, hi, fn, init):
     for i in range(lo, hi):
         fn(i, init)
+
+
+def spectrum_block(quads):
+    rows = []
+    for cc, cs, sc, ss in quads:
+        rows += [jnp.concatenate([cc, cs], axis=1), jnp.concatenate([sc, ss], axis=1)]
+    return split(jnp.concatenate(rows, axis=0))
 
 
 def kernel(
     mask, target, active, taps, weights, rh_in, rl_in, th_in, tl_in,
     gradient, resist,
     win, tapv, rh, rl, th, tl, targ, taph, rhat, xh, xl, mpart, hs, ms, vh, vl, amp, ph, pw,
-    ipart, ione, imid, itwo, resv, acc, tsend, tone, tmid, ttwo, gw, ecen, eside, outv,
+    ipart, ione, imid, itwo, acc, tsend, tone, tmid, ttwo, gw, ecen, eside,
     lsem, msend, mrecv, psend, precv, isend, isem, asend, asem, tss, trs, uss, urs, ess, ers,
 ):
     r, c, j = lax.axis_index("row"), lax.axis_index("col"), lax.axis_index("kern")
@@ -249,6 +251,7 @@
 
     def inverse_rows(a, carry):
         for b in range(2):
+            quads = []
             for f in range(2):
                 at = (slice(f * R, f * R + R), slice(b * R, b * R + R))
                 m = [ms[n, at[0], at[1]] for n in range(4)]
@@ -257,14 +260,9 @@
                 for n in (0, 2):
                     y.append(m[n] * h[n] + m[n + 1] * h[n + 1])
                     y.append(m[n + 1] * h[n] - m[n] * h[n + 1])
-                for n, x in enumerate(from_complex(*y)):
-                    h_, l_ = split(x)
-                    to = (slice(f * T + (n // 2) * R, f * T + (n // 2) * R + R),
-                          slice(b * T + (n % 2) * R, b * T + (n % 2) * R + R))
-                    xh[to[0], to[1]] = h_
-                    xl[to[0], to[1]] = l_
+                quads.append(from_complex(*y))
             at = slice(b * T, b * T + T)
-            h_, l_ = split(dot3(rh[:T, :], rl[:T, :], xh[:, at], xl[:, at]))
+            h_, l_ = split(dot3(rh[:T, :], rl[:T, :], *spectrum_block(quads)))
             vh[a, :, at] = h_
             vl[a, :, at] = l_
         return carry
@@ -315,7 +313,7 @@
             shares[2 * i + half].wait_recv()
         intensity = jnp.concatenate([imid[2 * i] + itwo[2 * i], imid[2 * i + 1] + itwo[2 * i + 1]], axis=1) * (1.0 / 12.0)
         x = 1.0 / (1.0 + jnp.exp(-8.0 * (intensity - 0.25)))
-        resv[at, :] = x
+        resist[at, :] = x
         factor = 2.0 * (x - targ[at, :].astype(F32)) * 8.0 * x * (1.0 - x)
         both = [split(factor * (weights[a % 3] * (2.0 / 12.0)) * amp[a, at, :]) for a in range(PARTS)]
         h_ = jnp.concatenate([x[0] for x in both], axis=0)
@@ -325,8 +323,6 @@
             u, v = split(dot3(h_, l_, rh[:T, cut], rl[:T, cut]).reshape(PARTS, Q, T))
             ph[:, at, cut] = u
             pw[:, at, cut] = v
-    store = pltpu.make_async_copy(resv, resist, lsem.at[7])
-    store.start()
 
     firsts = []
     for b in range(2):
@@ -345,15 +341,8 @@
             return carry
 
         loop(0, PARTS, gather, 0)
-        for f in range(2):
-            fr = slice(f * R, f * R + R)
-            for n, x in enumerate(from_complex(*[acc[i, fr, :] for i in range(4)])):
-                h_, l_ = split(x)
-                to = (slice(f * T + (n // 2) * R, f * T + (n // 2) * R + R),
-                      slice(b * T + (n % 2) * R, b * T + (n % 2) * R + R))
-                xh[to[0], to[1]] = h_
-                xl[to[0], to[1]] = l_
-        value = dot3(rh[...], rl[...], xh[:, at], xl[:, at])
+        quads = [from_complex(*[acc[i, f * R:f * R + R, :] for i in range(4)]) for f in range(2)]
+        value = dot3(rh[...], rl[...], *spectrum_block(quads))
         for q in range(4):
             for far in range(2):
                 m = (q + 6) % 8 if far == 0 else q + 2
@@ -407,11 +396,9 @@
     for n in range(5):
         pl.when(ends[n][1])(hops[n].wait_recv)
     own_part = gw[near_rows, mid] + ecen[...]
-    outv[:, :R] = (own_part[:, :R] + eside[1] + eside[3]) * pixels[:, :R]
-    outv[:, R:] = (own_part[:, R:] + eside[0] + eside[2]) * pixels[:, R:]
-
-    final = pltpu.make_async_copy(outv, gradient, lsem.at[0])
-    final.start()
+    gradient[:, :R] = (own_part[:, :R] + eside[1] + eside[3]) * pixels[:, :R]
+    gradient[:, R:] = (own_part[:, R:] + eside[0] + eside[2]) * pixels[:, R:]
+
 
     for n in range(8):
         pl.when(exists(*pieces[n][:2]))(copies[n].wait_send)
@@ -422,8 +409,6 @@
         copy.wait_send()
     for n in range(5):
         pl.when(ends[n][0])(hops[n].wait_send)
-    store.wait()
-    final.wait()
 
 
 def local(photomask, target_bits, active_blocks, kernel_taps, kernel_weights):
@@ -446,32 +431,28 @@
         vmem((PARTS, T, T), F32),
         vmem((PARTS, T, W), BF), vmem((PARTS, T, W), BF),
         vmem((4, Q, T), F32), vmem((8, Q, R), F32), vmem((8, Q, R), F32), vmem((8, Q, R), F32),
-        vmem((T, T), F32),
         vmem((4, T, R), F32),
         vmem((2, 4, 2, Q, T), F32),
         vmem((8, 2, Q, R), F32), vmem((4, 2, Q, R), F32), vmem((4, 2, Q, R), F32),
         vmem((2 * Q, W), F32),
         vmem((Q, T), F32), vmem((4, Q, R), F32),
-        vmem((Q, T), F32),
         dma((14,)), dma((8,)), dma((8,)),
         dma((6,)), dma((6,)),
         dma((8,)), dma((8,)), dma((8,)), dma((8,)),
         dma((8,)), dma((8,)), dma((4,)), dma((4,)),
         dma((5,)), dma((5,)),
     ]
-    outs = (jax.ShapeDtypeStruct((Q, T), F32), jax.ShapeDtypeStruct((T, T), F32))
-    gradient, resist = pl.pallas_call(
+    return pl.pallas_call(
         kernel,
-        out_shape=outs,
+        out_shape=(vmem((Q, T), F32), vmem((T, T), F32)),
         in_specs=[hbm, hbm, smem, hbm, smem, hbm, hbm, hbm, hbm],
-        out_specs=(hbm, hbm),
+        out_specs=(pl.BlockSpec(memory_space=vmem), pl.BlockSpec(memory_space=vmem)),
         scratch_shapes=scratch,
         compiler_params=pltpu.CompilerParams(
             collective_id=0, has_side_effects=True, vmem_limit_bytes=56 * 1024 * 1024),
         name="socs",
     )(photomask, target_bits, active_blocks, kernel_taps.transpose(1, 2, 0, 3), kernel_weights,
       *[jnp.asarray(t) for t in tables()])
-    return pl.pallas_call(hand_over, out_shape=outs, name="hand_over")(gradient, resist)
 
 
 def solution(mesh):

time: 55.6 us -> 54.3 us (0.977)
  Pallas kernels: 54.8 us -> 52.3 us
  local copies, waits for them, and re-layouts: 0 us -> 1.33 us
    pallas_call x2 -> x1, Pallas kernels: 54.8 us -> 52.3 us  [local(): pl.pallas_call(kernel, out_shape=(vmem((Q, T), F32), vmem((T, T), F32)),...]
    unnamed x0 -> x2, local copies, waits for them, and re-layouts: none -> 1.33 us
where the time goes in v5:
time: 54.3 us; the launch traced here: 54.2 us
  Pallas kernels  52.3 us (96%)
  local copies, waits for them, and re-layouts  1.33 us (2%)
  between operations  0.64 us (1%)
    pallas_call x1, Pallas kernels, local(): pl.pallas_call(kernel, out_shape=(vmem((Q, T), F32), vmem((T, T), F32)),...  52.3 us
    unnamed x2, local copies, waits for them, and re-layouts  1.33 us

profile of v5, /device:TPU:25, one launch (start us, length us, event | category | flops | bytes accessed | tf_op | source)
XLA Modules:
  0.0 54.2 jit_solution(9674581860629827588)
XLA Ops:
  0.6 52.3 %socs.1 = (f32[64,256]{1,0:T(8,128)S(1)}, f32[256,256]{1,0:T(8,128)S(1)}) custom-call(f32[256,256]{1,0:T(8,128)} %mask.1, s32[256,256]{1,0:T(8,128)} %target.1, s32[4,4]{1,0:T(4,128)} %active.1, f32[3,257,2,257]{3,2,1,0:T(2,128)} %bitcast.1, f32[3]{0:T(128)} %weights.1, bf16[512,512]{1,0:T(8,128)(2,1)} %constant.8.clone.rh_in, ...), custom_call_target="tpu_custom_call" | custom-call | tf_op jit(solution)/shard_map/socs/pallas_call | solution.py:445
  52.9 0.6 %copy.13 = f32[64,256]{1,0:T(8,128)} copy(f32[64,256]{1,0:T(8,128)S(1)} %get-tuple-element.2) | data formatting | bytes 131072
  53.5 0.7 %copy.14 = f32[256,256]{1,0:T(8,128)} copy(f32[256,256]{1,0:T(8,128)S(1)} %get-tuple-element.3) | data formatting | bytes 524288

commit v6 on v5

--- a/solution.py
+++ b/solution.py
@@ -290,10 +290,11 @@
     halves = (slice(0, R), slice(R, T))
     sums = []
     for i in range(4):
-        ipart[i] = amplitudes(i)
+        term = amplitudes(i)
         for half in range(2):
             n = 2 * i + half
-            copy = remote(ipart.at[i, :, halves[half]], ione.at[n], isend.at[n], isem.at[n], {"kern": pair[half]})
+            ipart[n] = term[:, halves[half]]
+            copy = remote(ipart.at[n], ione.at[n], isend.at[n], isem.at[n], {"kern": pair[half]})
             copy.start()
             sums.append(copy)
     shares = []
@@ -301,7 +302,7 @@
         for half in range(2):
             n = 2 * i + half
             sums[n].wait_recv()
-            imid[n] = ipart[i, :, halves[half]] + ione[n]
+            imid[n] = ipart[n] + ione[n]
             copy = remote(imid.at[n], itwo.at[n], asend.at[n], asem.at[n], {"kern": pair[1 - half]})
             copy.start()
             shares.append(copy)
@@ -324,10 +325,9 @@
             ph[:, at, cut] = u
             pw[:, at, cut] = v
 
-    firsts = []
+    firsts = [None] * 8
     for b in range(2):
         at = slice(b * T, b * T + T)
-        acc[...] = jnp.zeros_like(acc)
 
         def gather(a, carry, at=at, b=b):
             value = dot3(th[:, :T], tl[:, :T], ph[a, :, at], pw[a, :, at])
@@ -336,46 +336,48 @@
                 fr = slice(f * R, f * R + R)
                 h = [hs[a, n, fr, b * R:b * R + R] for n in range(4)]
                 for n in (0, 2):
-                    acc[n, fr, :] += p[n] * h[n] - p[n + 1] * h[n + 1]
-                    acc[n + 1, fr, :] += p[n] * h[n + 1] + p[n + 1] * h[n]
+                    for m, x in ((n, p[n] * h[n] - p[n + 1] * h[n + 1]), (n + 1, p[n] * h[n + 1] + p[n + 1] * h[n])):
+                        acc[m, fr, :] = x if a == 0 else acc[m, fr, :] + x
             return carry
 
         loop(0, PARTS, gather, 0)
         quads = [from_complex(*[acc[i, f * R:f * R + R, :] for i in range(4)]) for f in range(2)]
         value = dot3(rh[...], rl[...], *spectrum_block(quads))
-        for q in range(4):
-            for far in range(2):
-                m = (q + 6) % 8 if far == 0 else q + 2
-                tsend[b, q, far] = value[m * Q:m * Q + Q]
         for half in range(2):
-            to = pair[half]
-            for slot, owner in enumerate((to, partner(1 - half, to))):
-                n = (b * 2 + half) * 2 + slot
-                copy = remote(tsend.at[b, owner, :, :, half * R:half * R + R], tone.at[n],
-                              tss.at[n], trs.at[n], {"kern": to})
+            for q in range(4):
+                for far in range(2):
+                    m = (q + 6) % 8 if far == 0 else q + 2
+                    tsend[2 * b + half, q, far] = value[m * Q:m * Q + Q, half * R:half * R + R]
+        for kind in range(2):
+            for half in range(2):
+                n = 2 * b + half
+                to = pair[half]
+                owner = partner(1 - half, to) if kind == 0 else to
+                at = 4 * kind + n
+                copy = remote(tsend.at[n, owner], tone.at[at], tss.at[at], trs.at[at], {"kern": to})
                 copy.start()
-                firsts.append(copy)
+                firsts[at] = copy
 
     seconds = []
+    for n in range(4):
+        to = pair[1 - n % 2]
+        firsts[n].wait_recv()
+        tmid[n] = tsend[n, to] + tone[n]
+        copy = remote(tmid.at[n], ttwo.at[n], uss.at[n], urs.at[n], {"kern": to})
+        copy.start()
+        seconds.append(copy)
+
+    pixel_rows = None
     for b in range(2):
-        for half in range(2):
-            n = b * 2 + half
-            firsts[2 * n].wait_recv()
-            firsts[2 * n + 1].wait_recv()
-            to = pair[1 - half]
-            tmid[n] = tsend[b, to, :, :, half * R:half * R + R] + tone[2 * n + 1]
-            copy = remote(tmid.at[n], ttwo.at[n], uss.at[n], urs.at[n], {"kern": to})
-            copy.start()
-            seconds.append(copy)
-
-    for b in range(2):
-        for half in range(2):
-            n = b * 2 + half
+        parts = []
+        for n in (2 * b, 2 * b + 1):
+            firsts[4 + n].wait_recv()
             seconds[n].wait_recv()
-            part = tsend[b, j, :, :, half * R:half * R + R] + tone[2 * n] + ttwo[n]
-            gw[:, b * T + half * R:b * T + half * R + R] = part.reshape(2 * Q, R)
-    g_h, g_l = split(gw[...])
-    gw[...] = dot3(g_h, g_l, th[...], tl[...])
+            parts.append((tsend[n, j] + tone[4 + n] + ttwo[n]).reshape(2 * Q, R))
+        g_h, g_l = split(jnp.concatenate(parts, axis=1))
+        term = dot3(g_h, g_l, th[b * T:b * T + T, :], tl[b * T:b * T + T, :])
+        pixel_rows = term if b == 0 else pixel_rows + term
+    gw[...] = pixel_rows
     far_rows, near_rows = slice(0, Q), slice(Q, 2 * Q)
     west, east = exists(0, -1), exists(0, 1)
     ends = [
@@ -430,9 +432,9 @@
         vmem((PARTS, T, W), BF), vmem((PARTS, T, W), BF),
         vmem((PARTS, T, T), F32),
         vmem((PARTS, T, W), BF), vmem((PARTS, T, W), BF),
-        vmem((4, Q, T), F32), vmem((8, Q, R), F32), vmem((8, Q, R), F32), vmem((8, Q, R), F32),
+        vmem((8, Q, R), F32), vmem((8, Q, R), F32), vmem((8, Q, R), F32), vmem((8, Q, R), F32),
         vmem((4, T, R), F32),
-        vmem((2, 4, 2, Q, T), F32),
+        vmem((4, 4, 2, Q, R), F32),
         vmem((8, 2, Q, R), F32), vmem((4, 2, Q, R), F32), vmem((4, 2, Q, R), F32),
         vmem((2 * Q, W), F32),
         vmem((Q, T), F32), vmem((4, Q, R), F32),

time: 54.3 us -> 53.3 us (0.982)
  Pallas kernels: 52.3 us -> 51 us
    pallas_call x1, Pallas kernels: 52.3 us -> 51 us  [local(): pl.pallas_call(kernel, out_shape=(vmem((Q, T), F32), vmem((T, T), F32)),...]
where the time goes in v6:
time: 53.3 us; the launch traced here: 52.9 us
  Pallas kernels  51 us (96%)
  local copies, waits for them, and re-layouts  1.33 us (2%)
  between operations  0.64 us (1%)
    pallas_call x1, Pallas kernels, local(): pl.pallas_call(kernel, out_shape=(vmem((Q, T), F32), vmem((T, T), F32)),...  51 us
    unnamed x2, local copies, waits for them, and re-layouts  1.33 us

profile of v6, /device:TPU:25, one launch (start us, length us, event | category | flops | bytes accessed | tf_op | source)
XLA Modules:
  0.0 52.9 jit_solution(9343020213271908492)
XLA Ops:
  0.6 51.0 %socs.1 = (f32[64,256]{1,0:T(8,128)S(1)}, f32[256,256]{1,0:T(8,128)S(1)}) custom-call(f32[256,256]{1,0:T(8,128)} %mask.1, s32[256,256]{1,0:T(8,128)} %target.1, s32[4,4]{1,0:T(4,128)} %active.1, f32[3,257,2,257]{3,2,1,0:T(2,128)} %bitcast.1, f32[3]{0:T(128)} %weights.1, bf16[512,512]{1,0:T(8,128)(2,1)} %constant.8.clone.rh_in, ...), custom_call_target="tpu_custom_call" | custom-call | tf_op jit(solution)/shard_map/socs/pallas_call | solution.py:447
  51.6 0.6 %copy.13 = f32[64,256]{1,0:T(8,128)} copy(f32[64,256]{1,0:T(8,128)S(1)} %get-tuple-element.2) | data formatting | bytes 131072
  52.2 0.7 %copy.14 = f32[256,256]{1,0:T(8,128)} copy(f32[256,256]{1,0:T(8,128)S(1)} %get-tuple-element.3) | data formatting | bytes 524288

commit v7 on v6

--- a/solution.py
+++ b/solution.py
@@ -161,7 +161,7 @@
     ]
     copies = [remote(src, dst, msend.at[n], mrecv.at[n], device(dr, dc))
               for n, (dr, dc, src, dst) in enumerate(pieces)]
-    for n in range(8):
+    for n in range(4):
         pl.when(exists(*pieces[n][:2]))(copies[n].start)
 
     def arrived(n):
@@ -213,14 +213,16 @@
                     hs[a, n, f * R:f * R + R, b * R:b * R + R] = x
         return carry
 
-    loop(0, 4, tap_spectrum, 0)
+    for n in range(4, 8):
+        pl.when(exists(*pieces[n][:2]))(copies[n].start)
+    loop(0, 2, tap_spectrum, 0)
 
     for n in range(2):
         arrived(n)
         for d in range(3):
             pl.when(exists(-pieces[n][0], 0))(passes[d][n].start)
 
-    loop(4, PARTS, tap_spectrum, 0)
+    loop(2, PARTS, tap_spectrum, 0)
 
     loads[0].wait()
     for n in (2, 3):

time: 53.3 us -> 53.9 us (1.011); the launches traced: 52.9 us -> 52.9 us
  no operation moved by 1% of the time
where the time goes in v7:
time: 53.9 us; the launch traced here: 52.9 us
  Pallas kernels  51 us (95%)
  local copies, waits for them, and re-layouts  1.33 us (2%)
  between operations  0.64 us (1%)
    pallas_call x1, Pallas kernels, local(): pl.pallas_call(kernel, out_shape=(vmem((Q, T), F32), vmem((T, T), F32)),...  51 us
    unnamed x2, local copies, waits for them, and re-layouts  1.33 us

profile of v7, /device:TPU:25, one launch (start us, length us, event | category | flops | bytes accessed | tf_op | source)
XLA Modules:
  0.0 52.9 jit_solution(7384201253317583474)
XLA Ops:
  0.6 51.0 %socs.1 = (f32[64,256]{1,0:T(8,128)S(1)}, f32[256,256]{1,0:T(8,128)S(1)}) custom-call(f32[256,256]{1,0:T(8,128)} %mask.1, s32[256,256]{1,0:T(8,128)} %target.1, s32[4,4]{1,0:T(4,128)} %active.1, f32[3,257,2,257]{3,2,1,0:T(2,128)} %bitcast.1, f32[3]{0:T(128)} %weights.1, bf16[512,512]{1,0:T(8,128)(2,1)} %constant.8.clone.rh_in, ...), custom_call_target="tpu_custom_call" | custom-call | tf_op jit(solution)/shard_map/socs/pallas_call | solution.py:449
  51.6 0.6 %copy.13 = f32[64,256]{1,0:T(8,128)} copy(f32[64,256]{1,0:T(8,128)S(1)} %get-tuple-element.2) | data formatting | bytes 131072
  52.2 0.7 %copy.14 = f32[256,256]{1,0:T(8,128)} copy(f32[256,256]{1,0:T(8,128)S(1)} %get-tuple-element.3) | data formatting | bytes 524288

commit v8 on v6

--- a/solution.py
+++ b/solution.py
@@ -375,10 +375,14 @@
             seconds[n].wait_recv()
             parts.append((tsend[n, j] + tone[4 + n] + ttwo[n]).reshape(2 * Q, R))
         g_h, g_l = split(jnp.concatenate(parts, axis=1))
-        term = dot3(g_h, g_l, th[b * T:b * T + T, :], tl[b * T:b * T + T, :])
-        pixel_rows = term if b == 0 else pixel_rows + term
-    gw[...] = pixel_rows
+        if b == 0:
+            pixel_rows = dot3(g_h, g_l, th[:T, :], tl[:T, :])
     far_rows, near_rows = slice(0, Q), slice(Q, 2 * Q)
+
+    def last_block(at):
+        gw[at, :] = pixel_rows[at] + dot3(g_h[at], g_l[at], th[T:, :], tl[T:, :])
+
+    last_block(far_rows)
     west, east = exists(0, -1), exists(0, 1)
     ends = [
         (gives, takes, gw.at[far_rows, mid], ecen, device(step, 0)),
@@ -388,7 +392,10 @@
         (east, west, gw.at[near_rows, high], eside.at[3], device(0, 1)),
     ]
     hops = [remote(src, dst, ess.at[n], ers.at[n], to) for n, (_, _, src, dst, to) in enumerate(ends)]
-    for n in range(5):
+    for n in range(3):
+        pl.when(ends[n][0])(hops[n].start)
+    last_block(near_rows)
+    for n in range(3, 5):
         pl.when(ends[n][0])(hops[n].start)
     lane = lax.broadcasted_iota(jnp.int32, (1, T), 1) // 64
     pixels = jnp.zeros((1, T), F32)

time: 53.3 us -> 53.4 us (level)
  no operation moved by 1% of the time
where the time goes in v8:
time: 53.4 us; the launch traced here: 52.9 us
  Pallas kernels  51 us (96%)
  local copies, waits for them, and re-layouts  1.33 us (2%)
  between operations  0.64 us (1%)
    pallas_call x1, Pallas kernels, local(): pl.pallas_call(kernel, out_shape=(vmem((Q, T), F32), vmem((T, T), F32)),...  51 us
    unnamed x2, local copies, waits for them, and re-layouts  1.33 us

profile of v8, /device:TPU:25, one launch (start us, length us, event | category | flops | bytes accessed | tf_op | source)
XLA Modules:
  0.0 52.9 jit_solution(8006704638211337453)
XLA Ops:
  0.6 51.0 %socs.1 = (f32[64,256]{1,0:T(8,128)S(1)}, f32[256,256]{1,0:T(8,128)S(1)}) custom-call(f32[256,256]{1,0:T(8,128)} %mask.1, s32[256,256]{1,0:T(8,128)} %target.1, s32[4,4]{1,0:T(4,128)} %active.1, f32[3,257,2,257]{3,2,1,0:T(2,128)} %bitcast.1, f32[3]{0:T(128)} %weights.1, bf16[512,512]{1,0:T(8,128)(2,1)} %constant.8.clone.rh_in, ...), custom_call_target="tpu_custom_call" | custom-call | tf_op jit(solution)/shard_map/socs/pallas_call | solution.py:454
  51.6 0.6 %copy.13 = f32[64,256]{1,0:T(8,128)} copy(f32[64,256]{1,0:T(8,128)S(1)} %get-tuple-element.2) | data formatting | bytes 131072
  52.2 0.7 %copy.14 = f32[256,256]{1,0:T(8,128)} copy(f32[256,256]{1,0:T(8,128)S(1)} %get-tuple-element.3) | data formatting | bytes 524288
